TPU v7x, 128 devices: a whole 4x4x4 slice. The times are simulated.
128 devices in a mesh: seq: 32 (over z, x_hi, y), ch: 4 (over x_lo, core).
Axes of the slice: x: 4 (x_hi: 2, x_lo: 2; x = x_hi * 2 + x_lo), y: 4, z: 4, core: 2. Of those that a mesh axis runs over, the one named last changes fastest.
Arguments:
- tokens: bfloat16 [256, 512, 1536], P('seq', None, 'ch'), may hold values from -6 to 6
- gate_values: bfloat16 [256, 512, 1536], P('seq', None, 'ch'), may hold values from -6 to 6
- first_blocks: bfloat16 [256, 512, 512], P('seq'), may hold values from -0.25 to 0.25
- second_blocks: bfloat16 [512, 256, 256], P('seq'), may hold values from -0.375 to 0.375
- cotangent: bfloat16 [512, 256, 1536], P('seq', None, 'ch'), may hold values from -6 to 6
Outputs:
- mixed_output: bfloat16 [512, 256, 1536], P('seq', None, 'ch')
- token_grad: bfloat16 [256, 512, 1536], P('seq', None, 'ch')
- gate_grad: bfloat16 [256, 512, 1536], P('seq', None, 'ch')
- first_grad: bfloat16 [256, 512, 512], P('seq', 'ch')
- second_grad: bfloat16 [512, 256, 256], P(('seq', 'ch'))
All inputs are finite; a program needn't handle non-finite values.
Results may differ from a plain program's by a relative error of at most 0.013.
Values may be sent and summed in bfloat16 or wider, within the bound.
No kernel may reach another device: no remote copies, remote signals or barrier semaphores. Data moves between devices by JAX's collectives and lax.ppermute only.
A program may use at most 128 MiB of HBM per device.

v0:
```python
import jax
import jax.numpy as jnp
from jax import lax
from jax.sharding import PartitionSpec as P


def local(tokens, gate_values, first_blocks, second_blocks, cotangent):
    hidden = jnp.einsum("rpc,rcd->rpd", first_blocks, tokens, preferred_element_type=jnp.float32)
    gated_rows = (hidden * gate_values.astype(jnp.float32)).astype(jnp.bfloat16)
    grid_cols = lax.all_to_all(gated_rows, "seq", split_axis=1, concat_axis=0, tiled=True)
    mixed_output = jnp.einsum(
        "cqr,rcd->cqd", second_blocks, grid_cols, preferred_element_type=jnp.float32
    ).astype(jnp.bfloat16)
    second_terms = jnp.einsum(
        "cqd,rcd->cqr", cotangent, grid_cols, preferred_element_type=jnp.float32
    )
    second_grad = lax.psum_scatter(
        second_terms.astype(jnp.bfloat16), "ch", scatter_dimension=0, tiled=True
    )
    back_cols = jnp.einsum(
        "cqr,cqd->rcd", second_blocks, cotangent, preferred_element_type=jnp.float32
    ).astype(jnp.bfloat16)
    grad_rows = lax.all_to_all(back_cols, "seq", split_axis=0, concat_axis=1, tiled=True)
    grad_float = grad_rows.astype(jnp.float32)
    gate_grad = (grad_float * hidden).astype(jnp.bfloat16)
    hidden_grad = (grad_float * gate_values.astype(jnp.float32)).astype(jnp.bfloat16)
    token_grad = jnp.einsum(
        "rpc,rpd->rcd", first_blocks, hidden_grad, preferred_element_type=jnp.float32
    ).astype(jnp.bfloat16)
    first_terms = jnp.einsum(
        "rpd,rcd->rpc", hidden_grad, tokens, preferred_element_type=jnp.float32
    )
    first_grad = lax.psum_scatter(
        first_terms.astype(jnp.bfloat16), "ch", scatter_dimension=1, tiled=True
    )
    return (mixed_output, token_grad, gate_grad, first_grad, second_grad)


def solution(mesh):
    return jax.shard_map(
        local,
        mesh=mesh,
        in_specs=(
            P("seq", None, "ch"),
            P("seq", None, "ch"),
            P("seq", None, None),
            P("seq", None, None),
            P("seq", None, "ch"),
        ),
        out_specs=(
            P("seq", None, "ch"),
            P("seq", None, "ch"),
            P("seq", None, "ch"),
            P("seq", "ch", None),
            P(("seq", "ch"), None, None),
        ),
        check_vma=False,
    )
```

profile of v0, /device:TPU:1, one launch (start us, length us, event | category | flops | bytes accessed | tf_op | source)
XLA Modules:
  0.0 214.8 jit_solution(16979007219536640641)
XLA Ops:
  7.2 0.0 reduce-scatter.5.cloned.1.call-start
  7.2 5.4 %convert_bitcast_fusion.2 = bf16[256,16,384]{0,2,1:T(8,128)(2,1)} fusion(bf16[16,256,384]{2,1,0:T(8,128)(2,1)} %param.9, bf16[16,256,256]{2,1,0:T(8,128)(2,1)} %param.8), kind=kOutput, calls=%fused_computation.8 | convolution fusion | flops 806879232 | bytes 8388608 | tf_op jit(solution)/shard_map/cqr,cqd->rcd/dot_general | solution.py:20
  12.6 5.0 %copy.43 = bf16[256,16,384]{2,1,0:T(8,128)(2,1)} copy(bf16[256,16,384]{0,2,1:T(8,128)(2,1)} %convert_bitcast_fusion.2) | data formatting | bytes 6291456 | tf_op jit(solution)/shard_map/convert_element_type | solution.py:22
  17.6 50.7 %all_to_all.27 = bf16[256,16,384]{2,1,0:T(8,128)(2,1)S(1)} all-to-all(bf16[256,16,384]{2,1,0:T(8,128)(2,1)} %copy.43), channel_id=1, replica_groups=mesh['seq'=32,'ch'=4] {'seq'}, dimensions={0} | all-to-all | bytes 6291456 | tf_op jit(solution)/shard_map/all_to_all | solution.py:23
  68.3 0.8 convert_bitcast_fusion
  69.1 0.5 copy.44
  69.7 1.6 copy-done.1
  71.3 7.6 %fusion.2 = (bf16[8,512,384]{2,1,0:T(8,128)(2,1)}, bf16[8,512,384]{2,1,0:T(8,128)(2,1)}, bf16[8,512,384]{2,1,0:T(8,128)(2,1)S(1)}) fusion(f32[8,32,16,384]{3,2,1,0:T(8,128)S(1)} %copy.44, bf16[8,512,384]{2,1,0:T(8,128)(2,1)} %param.6, bf16[8,512,512]{2,1,0:T(8,128)(2,1)S(1)} %copy-done.1, bf16[8,512,384]{2,1,0:T(8,128)(2,1)S(1)} %copy-done), kind=kOutput, calls=%fused_computation.6 | convolution fusion | flops 1621622784 | bytes 26214400 | tf_op jit(solution)/shard_map/rpc,rcd->rpd/dot_general | solution.py:8
  78.9 1.9 copy.38
  80.8 45.2 %all_to_all.28 = bf16[8,512,384]{2,0,1:T(8,128)(2,1)S(1)} all-to-all(bf16[8,512,384]{2,0,1:T(8,128)(2,1)S(1)} %copy.38), channel_id=1, replica_groups=mesh['seq'=32,'ch'=4] {'seq'}, dimensions={1} | all-to-all | bytes 6291456 | tf_op jit(solution)/shard_map/all_to_all | solution.py:10
  126.0 0.7 copy.40
  126.7 1.7 copy-done.2
  128.4 0.2 copy-done.3
  128.6 2.7 %convert_bitcast_fusion.4 = bf16[16,256,256]{1,2,0:T(8,128)(2,1)} fusion(bf16[16,256,384]{2,1,0:T(8,128)(2,1)S(1)} %copy-done.3, bf16[256,16,384]{2,1,0:T(8,128)(2,1)S(1)} %bitcast.32), kind=kOutput, calls=%fused_computation.15 | convolution fusion | flops 806354944 | bytes 8388608 | tf_op jit(solution)/shard_map/cqd,rcd->cqr/dot_general | solution.py:14
  131.2 0.0 reduce-scatter.5.cloned.1.call-update
  131.3 0.2 reduce-scatter.3.cloned.1.call-start
  131.5 6.2 %convolution_convert_fusion = bf16[8,512,512]{2,1,0:T(8,128)(2,1)} fusion(bf16[8,512,384]{2,1,0:T(8,128)(2,1)} %get-tuple-element.26, bf16[8,512,384]{2,1,0:T(8,128)(2,1)S(1)} %copy-done), kind=kOutput, calls=%fused_computation.14 | convolution fusion | flops 1612709888 | bytes 10485760 | tf_op jit(solution)/shard_map/rpd,rcd->rpc/dot_general | solution.py:30
  137.7 0.0 reduce-scatter.3.cloned.1.call-update
  137.7 7.1 %convert_bitcast_fusion.1 = bf16[8,512,384]{1,2,0:T(8,128)(2,1)} fusion(bf16[8,512,384]{2,1,0:T(8,128)(2,1)} %get-tuple-element.26, bf16[8,512,512]{2,1,0:T(8,128)(2,1)} %param.7), kind=kOutput, calls=%fused_computation.7 | convolution fusion | flops 1612185600 | bytes 10485760 | tf_op jit(solution)/shard_map/rpc,rpd->rcd/dot_general | solution.py:27
  144.8 4.7 %copy.48 = bf16[8,512,384]{2,1,0:T(8,128)(2,1)} copy(bf16[8,512,384]{1,2,0:T(8,128)(2,1)} %convert_bitcast_fusion.1) | data formatting | bytes 6291456
  149.5 5.7 %convert_bitcast_fusion.3 = bf16[16,256,384]{1,2,0:T(8,128)(2,1)} fusion(bf16[16,256,256]{2,1,0:T(8,128)(2,1)} %param.8, bf16[256,16,384]{2,1,0:T(8,128)(2,1)} %bitcast.33), kind=kOutput, calls=%fused_computation.9 | convolution fusion | flops 806879232 | bytes 8388608 | tf_op jit(solution)/shard_map/cqr,rcd->cqd/dot_general | solution.py:11
  155.2 4.6 %copy.47 = bf16[16,256,384]{2,1,0:T(8,128)(2,1)} copy(bf16[16,256,384]{1,2,0:T(8,128)(2,1)} %convert_bitcast_fusion.3) | data formatting | bytes 6291456
  159.8 2.0 copy.49
  161.9 46.1 %reduce-scatter.3.cloned.1.call-done = bf16[8,128,512]{2,1,0:T(8,128)(2,1)} async-done(((bf16[8,512,512]{2,1,0:T(8,128)(2,1)}), bf16[8,128,512]{2,1,0:T(8,128)(2,1)}) %reduce-scatter.3.cloned.1.call-update) | async-done | bytes 1048592 | tf_op jit(solution)/shard_map/reduce_scatter | solution.py:33
  (6 shorter events, 0.0 us)
Async XLA Ops:
  7.2 62.5 %copy-start = (bf16[8,512,384]{2,1,0:T(8,128)(2,1)S(1)}, bf16[8,512,384]{2,1,0:T(8,128)(2,1)}, u32[]{:S(2)}) copy-start(bf16[8,512,384]{2,1,0:T(8,128)(2,1)} %param.5) | copy-start | bytes 9437188
  7.2 152.7 %reduce-scatter.5.cloned.1.call-start = ((), (), s32[]{:S(2)}) async-start(), calls=%async_computation.5 | async-start | bytes 2621440 | tf_op jit(solution)/shard_map/reduce_scatter | solution.py:17
  69.1 2.2 %copy-start.1 = (bf16[8,512,512]{2,1,0:T(8,128)(2,1)S(1)}, bf16[8,512,512]{2,1,0:T(8,128)(2,1)}, u32[]{:S(2)}) copy-start(bf16[8,512,512]{2,1,0:T(8,128)(2,1)} %param.7) | copy-start | bytes 12582916
  126.0 2.5 %copy-start.3 = (bf16[16,256,384]{2,1,0:T(8,128)(2,1)S(1)}, bf16[16,256,384]{2,1,0:T(8,128)(2,1)}, u32[]{:S(2)}) copy-start(bf16[16,256,384]{2,1,0:T(8,128)(2,1)} %param.9) | copy-start | bytes 9437188
  126.7 1.7 copy-start.2
  131.3 76.7 %reduce-scatter.3.cloned.1.call-start = ((), (), s32[]{:S(2)}) async-start(), calls=%async_computation.4 | async-start | bytes 5242880 | tf_op jit(solution)/shard_map/reduce_scatter | solution.py:33
Sparse Core Ops, SparseCore 0:
  131.4 27.0 reduce-scatter.4
  161.6 46.3 reduce-scatter.2
where the time goes:
time: 215 us
  blocking collectives  96 us (45%)
  waiting for transfers between devices  46.1 us (21%)
  matrix products  34.7 us (16%)
  local copies, waits for them, and re-layouts  22.8 us (11%)
  between operations  14.1 us (7%)
    all_to_all x1, blocking collectives, local(): lax.all_to_all(back_cols, 'seq', split_axis=0, concat_axis=1, tiled=True)  50.7 us
    reduce_scatter x1, waiting for transfers between devices, local(): lax.psum_scatter(first_terms.astype(jnp.bfloat16), 'ch', scatter_dimensio...  46.1 us
    all_to_all x1, blocking collectives, local(): lax.all_to_all(gated_rows, 'seq', split_axis=1, concat_axis=0, tiled=True)  45.2 us
    unnamed x11, local copies, waits for them, and re-layouts  14.8 us
    dot_general x1, matrix products, local(): jnp.einsum('rpc,rcd->rpd', first_blocks, tokens, preferred_element_type=j...  7.61 us
    dot_general x1, matrix products, local(): jnp.einsum('rpc,rpd->rcd', first_blocks, hidden_grad, preferred_element_t...  7.07 us
    dot_general x1, matrix products, local(): jnp.einsum('rpd,rcd->rpc', hidden_grad, tokens, preferred_element_type=jn...  6.2 us
    dot_general x1, matrix products, local(): jnp.einsum('cqr,rcd->cqd', second_blocks, grid_cols, preferred_element_ty...  5.72 us
  transfers between devices with their start and end apart: 2, of which 1 were waited for; matrix products, arithmetic and copies ran while one was open for 14% of the time, Pallas kernels for 0%

commit v1 on v0

v1 whole, which is shorter than its diff:
```python
import jax
import jax.numpy as jnp
from jax import lax
from jax.experimental import pallas as pl
from jax.experimental.pallas import tpu as pltpu
from jax.sharding import PartitionSpec as P

F32 = jnp.float32
BF16 = jnp.bfloat16
MIB = 1024 * 1024
LANES = 128
PAD = 8

NN = (((1,), (0,)), ((), ()))
NT = (((1,), (1,)), ((), ()))
TN = (((0,), (0,)), ((), ()))

HERE, ACROSS, BESIDE, OPPOSITE = range(4)

GRAD, GATED = range(2)


def dot(a, b, dims):
    return lax.dot_general(a, b, dims, preferred_element_type=F32)


def params(mib=60):
    return pltpu.CompilerParams(vmem_limit_bytes=mib * MIB)


def cost(flops, nbytes):
    return pl.CostEstimate(flops=flops, bytes_accessed=nbytes, transcendentals=0)


def lanes(t):
    return slice(t * LANES, (t + 1) * LANES)


def back_columns(second_blocks, cotangent, devices):
    cols, rows, d = cotangent.shape
    steps, tiles = 2, d // LANES
    span = rows // steps
    pitch = span + PAD
    per = rows // devices

    def kernel(s_ref, g_ref, out_ref, acc):
        for c in range(cols):
            back = dot(s_ref[c], g_ref[c], TN)
            for t in range(tiles):
                acc[t, c * pitch:c * pitch + span, :] = back[:, lanes(t)]

        def device(k, carry):
            for r in range(per):
                for t in range(tiles):
                    strip = acc[t, pl.ds(k * per + r, cols, stride=pitch), :]
                    out_ref[k, 0, r, :, lanes(t)] = strip.astype(BF16)
            return carry

        lax.fori_loop(0, span // per, device, 0, unroll=2)

    return pl.pallas_call(
        kernel,
        grid=(steps,),
        in_specs=[
            pl.BlockSpec((cols, rows, span), lambda i: (0, 0, i)),
            pl.BlockSpec((cols, rows, d), lambda i: (0, 0, 0)),
        ],
        out_specs=pl.BlockSpec((devices // steps, 1, per, cols, d), lambda i: (i, GRAD, 0, 0, 0)),
        out_shape=jax.ShapeDtypeStruct((devices, 2, per, cols, d), BF16),
        scratch_shapes=[pltpu.VMEM((tiles, cols * pitch, LANES), F32)],
        compiler_params=params(),
        cost_estimate=cost(2 * cols * rows * rows * d, 2 * cols * rows * (rows + 2 * d)),
    )(second_blocks, cotangent)


def gated_columns(first_blocks, tokens, gate_values, slabs):
    rows, cols, d = tokens.shape
    devices, _, pairs, both, _ = slabs.shape
    steps, tiles = 4, d // LANES
    span = cols // steps
    pitch = span + PAD

    def kernel(f_ref, t_ref, g_ref, _, out_ref, acc):
        for r in range(rows):
            gated = dot(f_ref[r], t_ref[r], NN) * g_ref[r].astype(F32)
            for t in range(tiles):
                acc[t, r * pitch:r * pitch + span, :] = gated[:, lanes(t)]

        def device(k, carry):
            for j in range(pairs):
                at = 2 * (k * pairs + j)
                for t in range(tiles):
                    even = acc[t, pl.ds(at, rows, stride=pitch), :]
                    odd = acc[t, pl.ds(at + 1, rows, stride=pitch), :]
                    out_ref[k, 0, j, :, lanes(t)] = jnp.concatenate([even, odd], axis=0).astype(BF16)
            return carry

        lax.fori_loop(0, devices // steps, device, 0)

    return pl.pallas_call(
        kernel,
        grid=(steps,),
        in_specs=[
            pl.BlockSpec((rows, span, cols), lambda i: (0, i, 0)),
            pl.BlockSpec((rows, cols, d), lambda i: (0, 0, 0)),
            pl.BlockSpec((rows, span, d), lambda i: (0, i, 0)),
            pl.BlockSpec(memory_space=pl.ANY),
        ],
        out_specs=pl.BlockSpec((devices // steps, 1, pairs, both, d), lambda i: (i, GATED, 0, 0, 0)),
        out_shape=jax.ShapeDtypeStruct(slabs.shape, BF16),
        scratch_shapes=[pltpu.VMEM((tiles, rows * pitch, LANES), F32)],
        input_output_aliases={3: 0},
        compiler_params=params(),
        cost_estimate=cost(2 * rows * cols * cols * d, 2 * rows * cols * (cols + 3 * d)),
    )(first_blocks, tokens, gate_values, slabs)


def grad_spec(slabs, first=0, step=1):
    devices, _, _, both, d = slabs.shape
    return pl.BlockSpec((devices, 1, step, both, d), lambda i: (0, GRAD, first + i, 0, 0))


def first_terms(place, slabs, tokens, gate_values, first, count):
    rows, cols, d = tokens.shape
    part = cols // 4

    def kernel(place_ref, b_ref, t_ref, g_ref, near_ref, far_ref, grad):
        group = b_ref.shape[0] // 4
        outs = (far_ref, far_ref, near_ref, near_ref)
        for k, whose in enumerate((BESIDE, OPPOSITE, HERE, ACROSS)):
            at = place_ref[whose]
            back = b_ref[pl.ds(at * group, group), 0, 0].reshape(part, d).astype(F32)
            gate = g_ref[0, pl.ds(pl.multiple_of(at * part, part), part), :].astype(F32)
            grad[k * part:(k + 1) * part, :] = (back * gate).astype(BF16)
        terms = dot(grad[...], t_ref[0], NT).astype(BF16)
        for k, out in enumerate(outs):
            out[k % 2, 0] = terms[k * part:(k + 1) * part]

    row_spec = pl.BlockSpec((1, cols, d), lambda i: (first + i, 0, 0))
    terms_spec = pl.BlockSpec((2, 1, part, cols), lambda i: (0, i, 0, 0))
    terms_shape = jax.ShapeDtypeStruct((2, count, part, cols), BF16)
    return pl.pallas_call(
        kernel,
        grid=(count,),
        in_specs=[pl.BlockSpec(memory_space=pltpu.SMEM), grad_spec(slabs, first), row_spec, row_spec],
        out_specs=[terms_spec, terms_spec],
        out_shape=[terms_shape, terms_shape],
        scratch_shapes=[pltpu.VMEM((cols, d), BF16)],
        compiler_params=params(24),
        cost_estimate=cost(2 * count * cols * cols * d, 2 * count * cols * (cols + 3 * d)),
    )(place, slabs, tokens, gate_values)


def row_grads(slabs, first_blocks, tokens, gate_values):
    rows, cols, d = tokens.shape

    step = 2

    def kernel(b_ref, f_ref, t_ref, g_ref, tg_ref, gg_ref):
        for k in range(step):
            back = b_ref[:, 0, k].reshape(cols, d).astype(F32)
            hidden_grad = (back * g_ref[k].astype(F32)).astype(BF16)
            tg_ref[k] = dot(f_ref[k], hidden_grad, TN).astype(BF16)
            gg_ref[k] = (back * dot(f_ref[k], t_ref[k], NN)).astype(BF16)

    row_spec = pl.BlockSpec((step, cols, d), lambda i: (i, 0, 0))
    row_shape = jax.ShapeDtypeStruct((rows, cols, d), BF16)
    return pl.pallas_call(
        kernel,
        grid=(rows // step,),
        in_specs=[grad_spec(slabs, 0, step), pl.BlockSpec((step, cols, cols), lambda i: (i, 0, 0)), row_spec, row_spec],
        out_specs=[row_spec, row_spec],
        out_shape=[row_shape, row_shape],
        compiler_params=params(24),
        cost_estimate=cost(4 * rows * cols * cols * d, 2 * rows * cols * (cols + 5 * d)),
    )(slabs, first_blocks, tokens, gate_values)


def column_pair(g_ref, k):
    devices, _, _, both, d = g_ref.shape
    pair = g_ref[:, 0, k].astype(F32).reshape(devices, 2, both // 2, d)
    return [pair[:, c].reshape(devices * both // 2, d).astype(BF16) for c in range(2)]


def second_terms(place, whose, slabs, cotangent):
    cols, rows, d = cotangent.shape
    devices, _, pairs, both, _ = slabs.shape
    step, part = pairs // 4, cols // 4

    def kernel(place_ref, g_ref, c_ref, out_ref):
        for k in range(step):
            for c, column in enumerate(column_pair(g_ref, k)):
                out_ref[0, 2 * k + c] = dot(c_ref[2 * k + c], column, NT).astype(BF16)

    def quarter(i, at):
        return jnp.where(i == 0, at[whose[0]], at[whose[1]])

    return pl.pallas_call(
        kernel,
        grid_spec=pltpu.PrefetchScalarGridSpec(
            num_scalar_prefetch=1,
            grid=(2,),
            in_specs=[
                pl.BlockSpec((devices, 1, step, both, d), lambda i, at: (0, GATED, quarter(i, at), 0, 0)),
                pl.BlockSpec((part, rows, d), lambda i, at: (quarter(i, at), 0, 0)),
            ],
            out_specs=pl.BlockSpec((1, part, rows, rows), lambda i, at: (i, 0, 0, 0)),
        ),
        out_shape=jax.ShapeDtypeStruct((2, part, rows, rows), BF16),
        compiler_params=params(24),
        cost_estimate=cost(cols * rows * rows * d, cols * rows * (rows + 2 * d)),
    )(place, slabs, cotangent)


def mixed_columns(slabs, second_blocks):
    cols, rows, _ = second_blocks.shape
    devices, _, pairs, both, d = slabs.shape
    step = 4

    def kernel(g_ref, s_ref, out_ref):
        for k in range(step):
            for c, column in enumerate(column_pair(g_ref, k)):
                out_ref[2 * k + c] = dot(s_ref[2 * k + c], column, NN).astype(BF16)

    return pl.pallas_call(
        kernel,
        grid=(pairs // step,),
        in_specs=[
            pl.BlockSpec((devices, 1, step, both, d), lambda i: (0, GATED, i, 0, 0)),
            pl.BlockSpec((2 * step, rows, rows), lambda i: (i, 0, 0)),
        ],
        out_specs=pl.BlockSpec((2 * step, rows, d), lambda i: (i, 0, 0)),
        out_shape=jax.ShapeDtypeStruct((cols, rows, d), BF16),
        compiler_params=params(24),
        cost_estimate=cost(2 * cols * rows * rows * d, 2 * cols * rows * (rows + 2 * d)),
    )(slabs, second_blocks)


def swap(x, bit):
    return lax.ppermute(x, "ch", [(i, i ^ bit) for i in range(4)])


def add(a, b):
    return a.astype(F32) + b.astype(F32)


def after(first, *later):
    return lax.optimization_barrier((first, *later))


def local(tokens, gate_values, first_blocks, second_blocks, cotangent):
    rows = tokens.shape[0]
    ch = lax.axis_index("ch")
    place = jnp.stack([ch, ch ^ 2, ch ^ 1, ch ^ 3]).astype(jnp.int32)

    slabs = back_columns(second_blocks, cotangent, lax.axis_size("seq"))
    slabs = gated_columns(first_blocks, tokens, gate_values, slabs)
    slabs, place = after(slabs, place)
    slabs = lax.all_to_all(slabs, "seq", split_axis=0, concat_axis=0, tiled=True)

    def over_cores(near, far):
        return add(near[1], far[1]).astype(BF16)

    def over_chips(near, far, across):
        return (add(near[0], far[0]) + across.astype(F32)).astype(BF16)

    few = rows // 4
    near_a, far_a = first_terms(place, slabs, tokens, gate_values, 0, few)
    far_a = swap(far_a, 1)
    far_c = swap(second_terms(place, (BESIDE, OPPOSITE), slabs, cotangent), 1)
    sum_a, cotangent = after(over_cores(near_a, far_a), cotangent)
    across_a = swap(sum_a, 2)
    near_c = second_terms(place, (HERE, ACROSS), slabs, cotangent)
    across_a, near_c = after(across_a, near_c)
    sum_c, tokens = after(over_cores(near_c, far_c), tokens)
    across_c = swap(sum_c, 2)
    near_b, far_b = first_terms(place, slabs, tokens, gate_values, few, rows - few)
    far_b = swap(far_b, 1)
    across_c, near_b = after(across_c, near_b)
    sum_b, gate_values, second_blocks = after(over_cores(near_b, far_b), gate_values, second_blocks)
    across_b = swap(sum_b, 2)
    mixed_output = mixed_columns(slabs, second_blocks)
    token_grad, gate_grad = row_grads(slabs, first_blocks, tokens, gate_values)
    first_grad = jnp.concatenate([over_chips(near_a, far_a, across_a), over_chips(near_b, far_b, across_b)], axis=0)
    second_grad = over_chips(near_c, far_c, across_c)
    return (mixed_output, token_grad, gate_grad, first_grad, second_grad)


def solution(mesh):
    return jax.shard_map(
        local,
        mesh=mesh,
        in_specs=(
            P("seq", None, "ch"),
            P("seq", None, "ch"),
            P("seq", None, None),
            P("seq", None, None),
            P("seq", None, "ch"),
        ),
        out_specs=(
            P("seq", None, "ch"),
            P("seq", None, "ch"),
            P("seq", None, "ch"),
            P("seq", "ch", None),
            P(("seq", "ch"), None, None),
        ),
        check_vma=False,
    )
```

time: 215 us -> 155 us (0.72)
  matrix products: 34.7 us -> 0 us
  Pallas kernels: 0 us -> 33.1 us
  local copies, waits for them, and re-layouts: 22.8 us -> 0.08 us
  waiting for transfers between devices: 46.1 us -> 27.4 us
  between operations: 14.1 us -> 0.71 us
  blocking collectives: 96 us -> 84.7 us
  starting transfers between devices: 0.26 us -> 5.59 us
  other arithmetic: 0.77 us -> 2.98 us
    reduce_scatter x2 -> x0, waiting for transfers between devices: 46.1 us -> none  [the longest x1 46.1 us: local(): lax.psum_scatter(first_terms.astype(jnp.bfloat16), 'ch', scatter_dimensio...]
    dot_general x6 -> x0, matrix products: 34.7 us -> none  [the longest x1 7.61 us: local(): jnp.einsum('rpc,rcd->rpd', first_blocks, tokens, preferred_element_type=j...]
    pallas_call x0 -> x8, Pallas kernels: none -> 33.1 us  [the longest x1 8.4 us: gated_columns(): pl.pallas_call(kernel, grid=(steps,), in_specs=[pl.BlockSpec((rows, span,...]
    ppermute x0 -> x6, waiting for transfers between devices: none -> 27.4 us  [swap(): return lax.ppermute(x, 'ch', [(i, i ^ bit) for i in range(4)])]
    unnamed x11 -> x10, local copies, waits for them, and re-layouts: 14.8 us -> 0.08 us
    all_to_all x2 -> x1, blocking collectives: 96 us -> 84.7 us  [local(): lax.all_to_all(slabs, 'seq', split_axis=0, concat_axis=0, tiled=True)]
    convert_element_type x3 -> x0, local copies, waits for them, and re-layouts: 7.35 us -> none  [the longest x1 4.96 us: local(): back_cols = jnp.einsum('cqr,cqd->rcd', second_blocks, cotangent, preferre...]
    ppermute x0 -> x6, starting transfers between devices: none -> 5.59 us  [swap(): return lax.ppermute(x, 'ch', [(i, i ^ bit) for i in range(4)])]
  transfers between devices with their start and end apart: 2 -> 6, of which waited for: 1 -> 4; matrix products, arithmetic and copies ran while one was open for 14% -> 1% of each run, Pallas kernels for 0% -> 8%
where the time goes in v1:
time: 155 us
  blocking collectives  84.7 us (55%)
  Pallas kernels  33.1 us (21%)
  waiting for transfers between devices  27.4 us (18%)
  starting transfers between devices  5.59 us (4%)
  other arithmetic  2.98 us (2%)
    all_to_all x1, blocking collectives, local(): lax.all_to_all(slabs, 'seq', split_axis=0, concat_axis=0, tiled=True)  84.7 us
    ppermute x6, waiting for transfers between devices, swap(): return lax.ppermute(x, 'ch', [(i, i ^ bit) for i in range(4)])  27.4 us
    pallas_call x1, Pallas kernels, gated_columns(): pl.pallas_call(kernel, grid=(steps,), in_specs=[pl.BlockSpec((rows, span,...  8.4 us
    pallas_call x1, Pallas kernels, row_grads(): pl.pallas_call(kernel, grid=(rows // step,), in_specs=[grad_spec(slabs, 0...  6.45 us
    pallas_call x1, Pallas kernels, back_columns(): pl.pallas_call(kernel, grid=(steps,), in_specs=[pl.BlockSpec((cols, rows,...  6.25 us
    pallas_call x2, Pallas kernels, first_terms(): pl.pallas_call(kernel, grid=(count,), in_specs=[pl.BlockSpec(memory_space...  5.74 us
    ppermute x6, starting transfers between devices, swap(): return lax.ppermute(x, 'ch', [(i, i ^ bit) for i in range(4)])  5.59 us
    pallas_call x2, Pallas kernels, second_terms(): pl.pallas_call(kernel, grid_spec=pltpu.PrefetchScalarGridSpec(num_scalar_...  3.4 us
  transfers between devices with their start and end apart: 6, of which 4 were waited for; matrix products, arithmetic and copies ran while one was open for 1% of the time, Pallas kernels for 8%

profile of v1, /device:TPU:1, one launch (start us, length us, event | category | flops | bytes accessed | tf_op | source)
XLA Modules:
  0.0 154.6 jit_solution(5987366546442198692)
XLA Ops:
  0.6 6.2 %shard_map.92._ = bf16[32,2,8,16,384]{4,3,2,1,0:T(8,128)(2,1)} custom-call(bf16[16,256,256]{2,1,0:T(8,128)(2,1)} %s_ref.2, bf16[16,256,384]{2,1,0:T(8,128)(2,1)} %c_ref.2), custom_call_target="tpu_custom_call" | custom-call | flops 805306368 | bytes 8388608 | tf_op jit(solution)/shard_map/pallas_call | solution.py:61
  7.0 8.4 %shard_map.93 = bf16[32,2,8,16,384]{4,3,2,1,0:T(8,128)(2,1)} custom-call(bf16[8,512,512]{2,1,0:T(8,128)(2,1)} %f_ref.3, bf16[8,512,384]{2,1,0:T(8,128)(2,1)} %t_ref.5, bf16[8,512,384]{2,1,0:T(8,128)(2,1)} %g_ref.8, bf16[32,2,8,16,384]{4,3,2,1,0:T(8,128)(2,1)} %shard_map.92._), custom_call_target="tpu_custom_call", output_to_operand_aliasing={{}: (3, {})} | custom-call | flops 1610612736 | bytes 13631488 | tf_op jit(solution)/shard_map/pallas_call | solution.py:100
  15.4 84.7 %all_to_all.5.b_ref.g_ref = bf16[32,2,8,16,384]{4,3,2,1,0:T(8,128)(2,1)S(1)} all-to-all(bf16[32,2,8,16,384]{4,3,2,1,0:T(8,128)(2,1)} %shard_map.93), channel_id=1, replica_groups=mesh['seq'=32,'ch'=4] {'seq'}, dimensions={0} | all-to-all | bytes 12582912 | tf_op jit(solution)/shard_map/all_to_all | solution.py:259
  100.1 1.7 %shard_map.96 = bf16[2,4,256,256]{3,2,1,0:T(8,128)(2,1)S(1)} custom-call(s32[4]{0:T(128)S(1)} %pad_add_fusion.place_ref, bf16[32,2,8,16,384]{4,3,2,1,0:T(8,128)(2,1)S(1)} %all_to_all.5.b_ref.g_ref, bf16[16,256,384]{2,1,0:T(8,128)(2,1)S(1)} %copy-done.2), custom_call_target="tpu_custom_call" | custom-call | flops 402653184 | bytes 4194304 | tf_op jit(solution)/shard_map/pallas_call | solution.py:198
  101.8 1.9 %collective-permute-start.2 = (bf16[2,4,256,256]{3,2,1,0:T(8,128)(2,1)S(1)}, bf16[2,4,256,256]{3,2,1,0:T(8,128)(2,1)S(1)}, u32[]{:S(2)}, u32[]{:S(2)}) collective-permute-start(bf16[2,4,256,256]{3,2,1,0:T(8,128)(2,1)S(1)} %shard_map.96), channel_id=1, source_target_pairs={{0,1},{1,0},{2,3},{3,2},{4,5},{5,4},{6,7},{7,6},{8,9},{9,8},{10,11... | collective-permute-start | bytes 3145736 | tf_op jit(solution)/shard_map/ppermute | solution.py:240
  103.7 1.7 %shard_map.94 = (bf16[2,2,128,512]{3,2,1,0:T(8,128)(2,1)S(1)}, bf16[2,2,128,512]{3,2,1,0:T(8,128)(2,1)S(1)}) custom-call(s32[4]{0:T(128)S(1)} %pad_add_fusion.place_ref, bf16[32,2,8,16,384]{4,3,2,1,0:T(8,128)(2,1)S(1)} %all_to_all.5.b_ref.g_ref, bf16[8,512,384]{2,1,0:T(8,128)(2,1)S(1)} %copy-done, bf16[8,512,384]{2,1,0:T(8,128)(2,1)S(1)} %copy-done.1), custom_call_target="tpu_custom_call" | custom-call | flops 402653184 | bytes 3407872 | tf_op jit(solution)/shard_map/pallas_call | solution.py:142
  105.4 1.1 collective-permute-start
  106.5 1.5 collective-permute-done
  108.2 0.4 collective-permute-start.1
  108.6 1.7 %shard_map.95 = bf16[2,4,256,256]{3,2,1,0:T(8,128)(2,1)S(1)} custom-call(s32[4]{0:T(128)S(1)} %pad_add_fusion.place_ref, bf16[32,2,8,16,384]{4,3,2,1,0:T(8,128)(2,1)S(1)} %all_to_all.5.b_ref.g_ref, bf16[16,256,384]{2,1,0:T(8,128)(2,1)S(1)} %copy-done.2), custom_call_target="tpu_custom_call" | custom-call | flops 402653184 | bytes 4194304 | tf_op jit(solution)/shard_map/pallas_call | solution.py:198
  110.3 5.5 %collective-permute-done.1 = bf16[2,128,512]{2,1,0:T(8,128)(2,1)S(1)} collective-permute-done((bf16[2,128,512]{2,1,0:T(8,128)(2,1)S(1)}, bf16[2,128,512]{2,1,0:T(8,128)(2,1)S(1)}, u32[]{:S(2)}, u32[]{:S(2)}) %collective-permute-start.1) | collective-permute-done | bytes 262176 | tf_op jit(solution)/shard_map/ppermute | solution.py:240
  115.8 0.1 fusion.3
  115.9 4.1 %shard_map.97 = (bf16[2,6,128,512]{3,2,1,0:T(8,128)(2,1)S(1)}, bf16[2,6,128,512]{3,2,1,0:T(8,128)(2,1)S(1)}) custom-call(s32[4]{0:T(128)S(1)} %pad_add_fusion.place_ref, bf16[32,2,8,16,384]{4,3,2,1,0:T(8,128)(2,1)S(1)} %all_to_all.5.b_ref.g_ref, bf16[8,512,384]{2,1,0:T(8,128)(2,1)S(1)} %copy-done, bf16[8,512,384]{2,1,0:T(8,128)(2,1)S(1)} %copy-done.1), custom_call_target="tpu_custom_call" | custom-call | flops 1207959552 | bytes 10223616 | tf_op jit(solution)/shard_map/pallas_call | solution.py:142
  120.0 1.3 collective-permute-start.4
  121.2 0.4 collective-permute-start.3
  121.6 13.1 %collective-permute-done.3 = bf16[4,256,256]{2,1,0:T(8,128)(2,1)S(1)} collective-permute-done((bf16[4,256,256]{2,1,0:T(8,128)(2,1)S(1)}, bf16[4,256,256]{2,1,0:T(8,128)(2,1)S(1)}, u32[]{:S(2)}, u32[]{:S(2)}) %collective-permute-start.3) | collective-permute-done | bytes 524320 | tf_op jit(solution)/shard_map/ppermute | solution.py:240
  134.7 0.2 fusion.2
  135.0 0.4 collective-permute-start.5
  135.5 1.0 fusion.1
  136.5 2.9 %shard_map.98 = bf16[16,256,384]{2,1,0:T(8,128)(2,1)} custom-call(bf16[32,2,8,16,384]{4,3,2,1,0:T(8,128)(2,1)S(1)} %all_to_all.5.b_ref.g_ref, bf16[16,256,256]{2,1,0:T(8,128)(2,1)S(1)} %copy-done.4), custom_call_target="tpu_custom_call" | custom-call | flops 805306368 | bytes 8388608 | tf_op jit(solution)/shard_map/pallas_call | solution.py:225
  139.4 6.4 %shard_map.99 = (bf16[8,512,384]{2,1,0:T(8,128)(2,1)}, bf16[8,512,384]{2,1,0:T(8,128)(2,1)}) custom-call(bf16[32,2,8,16,384]{4,3,2,1,0:T(8,128)(2,1)S(1)} %all_to_all.5.b_ref.g_ref, bf16[8,512,512]{2,1,0:T(8,128)(2,1)S(1)} %copy-done.3, bf16[8,512,384]{2,1,0:T(8,128)(2,1)S(1)} %copy-done, bf16[8,512,384]{2,1,0:T(8,128)(2,1)S(1)} %copy-done.1), custom_call_target="tpu_custom_call" | custom-call | flops 3221225472 | bytes 19922944 | tf_op jit(solution)/shard_map/pallas_call | solution.py:168
  145.9 7.3 %collective-permute-done.5 = bf16[6,128,512]{2,1,0:T(8,128)(2,1)S(1)} collective-permute-done((bf16[6,128,512]{2,1,0:T(8,128)(2,1)S(1)}, bf16[6,128,512]{2,1,0:T(8,128)(2,1)S(1)}, u32[]{:S(2)}, u32[]{:S(2)}) %collective-permute-start.5) | collective-permute-done | bytes 786464 | tf_op jit(solution)/shard_map/ppermute | solution.py:240
  153.2 0.3 fusion
  153.6 1.1 pad_maximum_fusion
  (15 shorter events, 0.3 us)
Async XLA Ops:
  15.4 84.7 %copy-start.2 = (bf16[16,256,384]{2,1,0:T(8,128)(2,1)S(1)}, bf16[16,256,384]{2,1,0:T(8,128)(2,1)}, u32[]{:S(2)}) copy-start(bf16[16,256,384]{2,1,0:T(8,128)(2,1)} %c_ref.2) | copy-start | bytes 9437188
  100.1 3.7 %copy-start = (bf16[8,512,384]{2,1,0:T(8,128)(2,1)S(1)}, bf16[8,512,384]{2,1,0:T(8,128)(2,1)}, u32[]{:S(2)}) copy-start(bf16[8,512,384]{2,1,0:T(8,128)(2,1)} %t_ref.5) | copy-start | bytes 9437188
  100.1 3.7 %copy-start.1 = (bf16[8,512,384]{2,1,0:T(8,128)(2,1)S(1)}, bf16[8,512,384]{2,1,0:T(8,128)(2,1)}, u32[]{:S(2)}) copy-start(bf16[8,512,384]{2,1,0:T(8,128)(2,1)} %g_ref.8) | copy-start | bytes 9437188
  101.8 14.0 %collective-permute-start.2 = (bf16[2,4,256,256]{3,2,1,0:T(8,128)(2,1)S(1)}, bf16[2,4,256,256]{3,2,1,0:T(8,128)(2,1)S(1)}, u32[]{:S(2)}, u32[]{:S(2)}) collective-permute-start(bf16[2,4,256,256]{3,2,1,0:T(8,128)(2,1)S(1)} %shard_map.96), channel_id=1, source_target_pairs={{0,1},{1,0},{2,3},{3,2},{4,5},{5,4},{6,7},{7,6},{8,9},{9,8},{10,11... | collective-permute-start | bytes 3145736 | tf_op jit(solution)/shard_map/ppermute | solution.py:240
  105.4 2.7 %collective-permute-start = (bf16[2,2,128,512]{3,2,1,0:T(8,128)(2,1)S(1)}, bf16[2,2,128,512]{3,2,1,0:T(8,128)(2,1)S(1)}, u32[]{:S(2)}, u32[]{:S(2)}) collective-permute-start(bf16[2,2,128,512]{3,2,1,0:T(8,128)(2,1)S(1)} %get-tuple-element.27), channel_id=1, source_target_pairs={{0,1},{1,0},{2,3},{3,2},{4,5},{5,4},{6,7},{7,6},{8,9},{9,8},{10,11... | collective-permute-start | bytes 1572872 | tf_op jit(solution)/shard_map/ppermute | solution.py:240
  108.2 7.6 %collective-permute-start.1 = (bf16[2,128,512]{2,1,0:T(8,128)(2,1)S(1)}, bf16[2,128,512]{2,1,0:T(8,128)(2,1)S(1)}, u32[]{:S(2)}, u32[]{:S(2)}) collective-permute-start(bf16[2,128,512]{2,1,0:T(8,128)(2,1)S(1)} %fusion.5), channel_id=1, source_target_pairs={{0,2},{1,3},{2,0},{3,1},{4,6},{5,7},{6,4},{7,5},{8,10},{9,11},{10,... | collective-permute-start | bytes 786440 | tf_op jit(solution)/shard_map/ppermute | solution.py:240
  120.0 14.8 %collective-permute-start.4 = (bf16[2,6,128,512]{3,2,1,0:T(8,128)(2,1)S(1)}, bf16[2,6,128,512]{3,2,1,0:T(8,128)(2,1)S(1)}, u32[]{:S(2)}, u32[]{:S(2)}) collective-permute-start(bf16[2,6,128,512]{3,2,1,0:T(8,128)(2,1)S(1)} %get-tuple-element.35), channel_id=1, source_target_pairs={{0,1},{1,0},{2,3},{3,2},{4,5},{5,4},{6,7},{7,6},{8,9},{9,8},{10,11... | collective-permute-start | bytes 4718600 | tf_op jit(solution)/shard_map/ppermute | solution.py:240
  121.2 13.5 %collective-permute-start.3 = (bf16[4,256,256]{2,1,0:T(8,128)(2,1)S(1)}, bf16[4,256,256]{2,1,0:T(8,128)(2,1)S(1)}, u32[]{:S(2)}, u32[]{:S(2)}) collective-permute-start(bf16[4,256,256]{2,1,0:T(8,128)(2,1)S(1)} %fusion.3), channel_id=1, source_target_pairs={{0,2},{1,3},{2,0},{3,1},{4,6},{5,7},{6,4},{7,5},{8,10},{9,11},{10,... | collective-permute-start | bytes 1572872 | tf_op jit(solution)/shard_map/ppermute | solution.py:240
  135.0 1.6 %copy-start.4 = (bf16[16,256,256]{2,1,0:T(8,128)(2,1)S(1)}, bf16[16,256,256]{2,1,0:T(8,128)(2,1)}, u32[]{:S(2)}) copy-start(bf16[16,256,256]{2,1,0:T(8,128)(2,1)} %s_ref.2) | copy-start | bytes 6291460
  135.0 18.3 %collective-permute-start.5 = (bf16[6,128,512]{2,1,0:T(8,128)(2,1)S(1)}, bf16[6,128,512]{2,1,0:T(8,128)(2,1)S(1)}, u32[]{:S(2)}, u32[]{:S(2)}) collective-permute-start(bf16[6,128,512]{2,1,0:T(8,128)(2,1)S(1)} %fusion.2), channel_id=1, source_target_pairs={{0,2},{1,3},{2,0},{3,1},{4,6},{5,7},{6,4},{7,5},{8,10},{9,11},{10,... | collective-permute-start | bytes 2359304 | tf_op jit(solution)/shard_map/ppermute | solution.py:240
  136.5 2.9 %copy-start.3 = (bf16[8,512,512]{2,1,0:T(8,128)(2,1)S(1)}, bf16[8,512,512]{2,1,0:T(8,128)(2,1)}, u32[]{:S(2)}) copy-start(bf16[8,512,512]{2,1,0:T(8,128)(2,1)} %f_ref.3) | copy-start | bytes 12582916

commit v2 on v1

--- a/solution.py
+++ b/solution.py
@@ -36,83 +36,88 @@
     return slice(t * LANES, (t + 1) * LANES)
 
 
-def back_columns(second_blocks, cotangent, devices):
-    cols, rows, d = cotangent.shape
-    steps, tiles = 2, d // LANES
-    span = rows // steps
-    pitch = span + PAD
-    per = rows // devices
-
-    def kernel(s_ref, g_ref, out_ref, acc):
-        for c in range(cols):
-            back = dot(s_ref[c], g_ref[c], TN)
+def send_slabs(second_blocks, cotangent, first_blocks, tokens, gate_values, devices):
+    cols, all_rows, d = cotangent.shape
+    rows, all_cols, _ = tokens.shape
+    tiles, pairs = d // LANES, cols // 2
+    chunk = 4
+    chunks = cols // chunk
+    back_pitch, gated_pitch = all_rows + PAD, all_cols + PAD
+
+    def kernel(s_hbm, c_hbm, f_hbm, t_hbm, g_hbm, out_ref, s_ref, c_ref, f_ref, t_ref, g_ref, back, gated, sems):
+        fetches = []
+
+        def fetch(first, count, *pairs_of_refs):
+            for source, target in pairs_of_refs:
+                at = pl.ds(first, count)
+                copy = pltpu.make_async_copy(source.at[at], target.at[at], sems.at[len(fetches)])
+                copy.start()
+                fetches.append(copy)
+
+        def arrive(first, count):
+            for copy in fetches[first:first + count]:
+                copy.wait()
+
+        for i in range(chunks):
+            fetch(i * chunk, chunk, (s_hbm, s_ref), (c_hbm, c_ref))
+        for r in range(rows):
+            fetch(r, 1, (f_hbm, f_ref), (t_hbm, t_ref), (g_hbm, g_ref))
+
+        for i in range(chunks):
+            arrive(2 * i, 2)
+            for c in range(i * chunk, (i + 1) * chunk):
+                product = dot(s_ref[c], c_ref[c], TN)
+                for t in range(tiles):
+                    back[t, c * back_pitch:c * back_pitch + all_rows, :] = product[:, lanes(t)]
+
+        def rows_of(k, carry):
+            for r in range(rows):
+                for t in range(tiles):
+                    strip = back[t, pl.ds(k * rows + r, cols, stride=back_pitch), :]
+                    out_ref[k, GRAD, r, :, lanes(t)] = strip.astype(BF16)
+            return carry
+
+        lax.fori_loop(0, devices, rows_of, 0, unroll=2)
+
+        for r in range(rows):
+            arrive(2 * chunks + 3 * r, 3)
+            product = dot(f_ref[r], t_ref[r], NN) * g_ref[r].astype(F32)
             for t in range(tiles):
-                acc[t, c * pitch:c * pitch + span, :] = back[:, lanes(t)]
-
-        def device(k, carry):
-            for r in range(per):
+                gated[t, r * gated_pitch:r * gated_pitch + all_cols, :] = product[:, lanes(t)]
+
+        def columns_of(k, carry):
+            for j in range(pairs):
+                at = k * cols + 2 * j
                 for t in range(tiles):
-                    strip = acc[t, pl.ds(k * per + r, cols, stride=pitch), :]
-                    out_ref[k, 0, r, :, lanes(t)] = strip.astype(BF16)
+                    even = gated[t, pl.ds(at, rows, stride=gated_pitch), :]
+                    odd = gated[t, pl.ds(at + 1, rows, stride=gated_pitch), :]
+                    out_ref[k, GATED, j, :, lanes(t)] = jnp.concatenate([even, odd], axis=0).astype(BF16)
             return carry
 
-        lax.fori_loop(0, span // per, device, 0, unroll=2)
-
-    return pl.pallas_call(
-        kernel,
-        grid=(steps,),
-        in_specs=[
-            pl.BlockSpec((cols, rows, span), lambda i: (0, 0, i)),
-            pl.BlockSpec((cols, rows, d), lambda i: (0, 0, 0)),
+        lax.fori_loop(0, devices, columns_of, 0, unroll=2)
+
+    hbm = pl.BlockSpec(memory_space=pltpu.HBM)
+    return pl.pallas_call(
+        kernel,
+        in_specs=[hbm] * 5,
+        out_specs=pl.BlockSpec(memory_space=pltpu.VMEM),
+        out_shape=pltpu.VMEM((devices, 2, rows, cols, d), BF16),
+        scratch_shapes=[
+            pltpu.VMEM(second_blocks.shape, BF16),
+            pltpu.VMEM(cotangent.shape, BF16),
+            pltpu.VMEM(first_blocks.shape, BF16),
+            pltpu.VMEM(tokens.shape, BF16),
+            pltpu.VMEM(gate_values.shape, BF16),
+            pltpu.VMEM((tiles, cols * back_pitch, LANES), F32),
+            pltpu.VMEM((tiles, rows * gated_pitch, LANES), F32),
+            pltpu.SemaphoreType.DMA((2 * chunks + 3 * rows,)),
         ],
-        out_specs=pl.BlockSpec((devices // steps, 1, per, cols, d), lambda i: (i, GRAD, 0, 0, 0)),
-        out_shape=jax.ShapeDtypeStruct((devices, 2, per, cols, d), BF16),
-        scratch_shapes=[pltpu.VMEM((tiles, cols * pitch, LANES), F32)],
-        compiler_params=params(),
-        cost_estimate=cost(2 * cols * rows * rows * d, 2 * cols * rows * (rows + 2 * d)),
-    )(second_blocks, cotangent)
-
-
-def gated_columns(first_blocks, tokens, gate_values, slabs):
-    rows, cols, d = tokens.shape
-    devices, _, pairs, both, _ = slabs.shape
-    steps, tiles = 4, d // LANES
-    span = cols // steps
-    pitch = span + PAD
-
-    def kernel(f_ref, t_ref, g_ref, _, out_ref, acc):
-        for r in range(rows):
-            gated = dot(f_ref[r], t_ref[r], NN) * g_ref[r].astype(F32)
-            for t in range(tiles):
-                acc[t, r * pitch:r * pitch + span, :] = gated[:, lanes(t)]
-
-        def device(k, carry):
-            for j in range(pairs):
-                at = 2 * (k * pairs + j)
-                for t in range(tiles):
-                    even = acc[t, pl.ds(at, rows, stride=pitch), :]
-                    odd = acc[t, pl.ds(at + 1, rows, stride=pitch), :]
-                    out_ref[k, 0, j, :, lanes(t)] = jnp.concatenate([even, odd], axis=0).astype(BF16)
-            return carry
-
-        lax.fori_loop(0, devices // steps, device, 0)
-
-    return pl.pallas_call(
-        kernel,
-        grid=(steps,),
-        in_specs=[
-            pl.BlockSpec((rows, span, cols), lambda i: (0, i, 0)),
-            pl.BlockSpec((rows, cols, d), lambda i: (0, 0, 0)),
-            pl.BlockSpec((rows, span, d), lambda i: (0, i, 0)),
-            pl.BlockSpec(memory_space=pl.ANY),
-        ],
-        out_specs=pl.BlockSpec((devices // steps, 1, pairs, both, d), lambda i: (i, GATED, 0, 0, 0)),
-        out_shape=jax.ShapeDtypeStruct(slabs.shape, BF16),
-        scratch_shapes=[pltpu.VMEM((tiles, rows * pitch, LANES), F32)],
-        input_output_aliases={3: 0},
-        compiler_params=params(),
-        cost_estimate=cost(2 * rows * cols * cols * d, 2 * rows * cols * (cols + 3 * d)),
-    )(first_blocks, tokens, gate_values, slabs)
+        compiler_params=params(48),
+        cost_estimate=cost(
+            2 * cols * all_rows * all_rows * d + 2 * rows * all_cols * all_cols * d,
+            2 * cols * all_rows * (all_rows + 2 * d) + 2 * rows * all_cols * (all_cols + 3 * d),
+        ),
+    )(second_blocks, cotangent, first_blocks, tokens, gate_values)
 
 
 def grad_spec(slabs, first=0, step=1):
@@ -253,8 +258,7 @@
     ch = lax.axis_index("ch")
     place = jnp.stack([ch, ch ^ 2, ch ^ 1, ch ^ 3]).astype(jnp.int32)
 
-    slabs = back_columns(second_blocks, cotangent, lax.axis_size("seq"))
-    slabs = gated_columns(first_blocks, tokens, gate_values, slabs)
+    slabs = send_slabs(second_blocks, cotangent, first_blocks, tokens, gate_values, lax.axis_size("seq"))
     slabs, place = after(slabs, place)
     slabs = lax.all_to_all(slabs, "seq", split_axis=0, concat_axis=0, tiled=True)
 
@@ -264,25 +268,16 @@
     def over_chips(near, far, across):
         return (add(near[0], far[0]) + across.astype(F32)).astype(BF16)
 
-    few = rows // 4
-    near_a, far_a = first_terms(place, slabs, tokens, gate_values, 0, few)
-    far_a = swap(far_a, 1)
+    near_b, far_b = first_terms(place, slabs, tokens, gate_values, 0, rows)
+    far_b = swap(far_b, 1)
     far_c = swap(second_terms(place, (BESIDE, OPPOSITE), slabs, cotangent), 1)
-    sum_a, cotangent = after(over_cores(near_a, far_a), cotangent)
-    across_a = swap(sum_a, 2)
     near_c = second_terms(place, (HERE, ACROSS), slabs, cotangent)
-    across_a, near_c = after(across_a, near_c)
-    sum_c, tokens = after(over_cores(near_c, far_c), tokens)
-    across_c = swap(sum_c, 2)
-    near_b, far_b = first_terms(place, slabs, tokens, gate_values, few, rows - few)
-    far_b = swap(far_b, 1)
-    across_c, near_b = after(across_c, near_b)
-    sum_b, gate_values, second_blocks = after(over_cores(near_b, far_b), gate_values, second_blocks)
-    across_b = swap(sum_b, 2)
+    sum_b, sum_c = over_cores(near_b, far_b), over_cores(near_c, far_c)
+    sum_b, sum_c, gate_values, second_blocks = after(sum_b, sum_c, gate_values, second_blocks)
+    across_b, across_c = swap(sum_b, 2), swap(sum_c, 2)
     mixed_output = mixed_columns(slabs, second_blocks)
     token_grad, gate_grad = row_grads(slabs, first_blocks, tokens, gate_values)
-    first_grad = jnp.concatenate([over_chips(near_a, far_a, across_a), over_chips(near_b, far_b, across_b)], axis=0)
-    second_grad = over_chips(near_c, far_c, across_c)
+    first_grad, second_grad = over_chips(near_b, far_b, across_b), over_chips(near_c, far_c, across_c)
     return (mixed_output, token_grad, gate_grad, first_grad, second_grad)
 
 

time: 155 us -> 146 us (0.942)
  Pallas kernels: 33.1 us -> 27.5 us
  starting transfers between devices: 5.59 us -> 3.6 us
    pallas_call x2 -> x1, Pallas kernels: 14.6 us -> 9.57 us  [send_slabs(): pl.pallas_call(kernel, in_specs=[hbm] * 5, out_specs=pl.BlockSpec(memory_...]
    ppermute x6 -> x4, starting transfers between devices: 5.59 us -> 3.6 us  [swap(): return lax.ppermute(x, 'ch', [(i, i ^ bit) for i in range(4)])]
    ppermute x6 -> x4, waiting for transfers between devices: 27.4 us -> 26.5 us  [swap(): return lax.ppermute(x, 'ch', [(i, i ^ bit) for i in range(4)])]
    pallas_call x2 -> x1, Pallas kernels: 5.74 us -> 5.23 us  [first_terms(): pl.pallas_call(kernel, grid=(count,), in_specs=[pl.BlockSpec(memory_space...]
  transfers between devices with their start and end apart: 6 -> 4, of which waited for: 4 -> 2; matrix products, arithmetic and copies ran while one was open for 1% -> 1% of each run, Pallas kernels for 8% -> 9%
where the time goes in v2:
time: 146 us
  blocking collectives  84.5 us (58%)
  Pallas kernels  27.5 us (19%)
  waiting for transfers between devices  26.5 us (18%)
  starting transfers between devices  3.6 us (2%)
  other arithmetic  2.98 us (2%)
    all_to_all x1, blocking collectives, local(): lax.all_to_all(slabs, 'seq', split_axis=0, concat_axis=0, tiled=True)  84.5 us
    ppermute x4, waiting for transfers between devices, swap(): return lax.ppermute(x, 'ch', [(i, i ^ bit) for i in range(4)])  26.5 us
    pallas_call x1, Pallas kernels, send_slabs(): pl.pallas_call(kernel, in_specs=[hbm] * 5, out_specs=pl.BlockSpec(memory_...  9.57 us
    pallas_call x1, Pallas kernels, row_grads(): pl.pallas_call(kernel, grid=(rows // step,), in_specs=[grad_spec(slabs, 0...  6.45 us
    pallas_call x1, Pallas kernels, first_terms(): pl.pallas_call(kernel, grid=(count,), in_specs=[pl.BlockSpec(memory_space...  5.23 us
    ppermute x4, starting transfers between devices, swap(): return lax.ppermute(x, 'ch', [(i, i ^ bit) for i in range(4)])  3.6 us
    pallas_call x2, Pallas kernels, second_terms(): pl.pallas_call(kernel, grid_spec=pltpu.PrefetchScalarGridSpec(num_scalar_...  3.41 us
  transfers between devices with their start and end apart: 4, of which 2 were waited for; matrix products, arithmetic and copies ran while one was open for 1% of the time, Pallas kernels for 9%

profile of v2, /device:TPU:1, one launch (start us, length us, event | category | flops | bytes accessed | tf_op | source)
XLA Modules:
  0.0 145.9 jit_solution(5013975434454287284)
XLA Ops:
  0.6 0.1 pad_add_fusion.place_ref
  0.7 9.6 %shard_map.92 = bf16[32,2,8,16,384]{4,3,2,1,0:T(8,128)(2,1)S(1)} custom-call(bf16[16,256,256]{2,1,0:T(8,128)(2,1)} %s_ref, bf16[16,256,384]{2,1,0:T(8,128)(2,1)} %c_ref.3, bf16[8,512,512]{2,1,0:T(8,128)(2,1)} %f_ref.1, bf16[8,512,384]{2,1,0:T(8,128)(2,1)} %t_ref.3, bf16[8,512,384]{2,1,0:T(8,128)(2,1)} %g_ref.2), custom_call_target="tpu_custom_call" | custom-call | flops 2415919104 | bytes 22020096 | tf_op jit(solution)/shard_map/pallas_call | solution.py:100
  10.3 0.0 copy-start
  10.3 0.0 copy-start.1
  10.3 84.5 %all_to_all.5.b_ref.g_ref = bf16[32,2,8,16,384]{4,3,2,1,0:T(8,128)(2,1)S(1)} all-to-all(bf16[32,2,8,16,384]{4,3,2,1,0:T(8,128)(2,1)S(1)} %shard_map.92), channel_id=1, replica_groups=mesh['seq'=32,'ch'=4] {'seq'}, dimensions={0} | all-to-all | bytes 12582912 | tf_op jit(solution)/shard_map/all_to_all | solution.py:263
  94.8 0.0 copy-done.1
  94.8 5.2 %shard_map.93 = (bf16[2,8,128,512]{3,2,1,0:T(8,128)(2,1)S(1)}, bf16[2,8,128,512]{3,2,1,0:T(8,128)(2,1)S(1)}) custom-call(s32[4]{0:T(128)S(1)} %pad_add_fusion.place_ref, bf16[32,2,8,16,384]{4,3,2,1,0:T(8,128)(2,1)S(1)} %all_to_all.5.b_ref.g_ref, bf16[8,512,384]{2,1,0:T(8,128)(2,1)S(1)} %copy-done, bf16[8,512,384]{2,1,0:T(8,128)(2,1)S(1)} %copy-done.1), custom_call_target="tpu_custom_call" | custom-call | flops 1610612736 | bytes 13631488 | tf_op jit(solution)/shard_map/pallas_call | solution.py:147
  100.1 2.0 %collective-permute-start = (bf16[2,8,128,512]{3,2,1,0:T(8,128)(2,1)S(1)}, bf16[2,8,128,512]{3,2,1,0:T(8,128)(2,1)S(1)}, u32[]{:S(2)}, u32[]{:S(2)}) collective-permute-start(bf16[2,8,128,512]{3,2,1,0:T(8,128)(2,1)S(1)} %get-tuple-element.18), channel_id=1, source_target_pairs={{0,1},{1,0},{2,3},{3,2},{4,5},{5,4},{6,7},{7,6},{8,9},{9,8},{10,11... | collective-permute-start | bytes 6291464 | tf_op jit(solution)/shard_map/ppermute | solution.py:245
  102.0 1.7 %shard_map.95 = bf16[2,4,256,256]{3,2,1,0:T(8,128)(2,1)S(1)} custom-call(s32[4]{0:T(128)S(1)} %pad_add_fusion.place_ref, bf16[32,2,8,16,384]{4,3,2,1,0:T(8,128)(2,1)S(1)} %all_to_all.5.b_ref.g_ref, bf16[16,256,384]{2,1,0:T(8,128)(2,1)S(1)} %copy-done.2), custom_call_target="tpu_custom_call" | custom-call | flops 402653184 | bytes 4194304 | tf_op jit(solution)/shard_map/pallas_call | solution.py:203
  103.7 0.1 collective-permute-start.1
  103.8 1.7 %shard_map.94 = bf16[2,4,256,256]{3,2,1,0:T(8,128)(2,1)S(1)} custom-call(s32[4]{0:T(128)S(1)} %pad_add_fusion.place_ref, bf16[32,2,8,16,384]{4,3,2,1,0:T(8,128)(2,1)S(1)} %all_to_all.5.b_ref.g_ref, bf16[16,256,384]{2,1,0:T(8,128)(2,1)S(1)} %copy-done.2), custom_call_target="tpu_custom_call" | custom-call | flops 402653184 | bytes 4194304 | tf_op jit(solution)/shard_map/pallas_call | solution.py:203
  105.5 0.0 copy-start.4
  105.6 1.7 %collective-permute-done.1 = bf16[2,4,256,256]{3,2,1,0:T(8,128)(2,1)S(1)} collective-permute-done((bf16[2,4,256,256]{3,2,1,0:T(8,128)(2,1)S(1)}, bf16[2,4,256,256]{3,2,1,0:T(8,128)(2,1)S(1)}, u32[]{:S(2)}, u32[]{:S(2)}) %collective-permute-start.1) | collective-permute-done | bytes 1048608 | tf_op jit(solution)/shard_map/ppermute | solution.py:245
  107.3 0.1 fusion.3
  107.4 0.0 collective-permute-done
  107.5 0.3 fusion.1
  107.8 0.4 collective-permute-start.2
  108.2 1.1 collective-permute-start.3
  109.3 2.9 %shard_map.96 = bf16[16,256,384]{2,1,0:T(8,128)(2,1)} custom-call(bf16[32,2,8,16,384]{4,3,2,1,0:T(8,128)(2,1)S(1)} %all_to_all.5.b_ref.g_ref, bf16[16,256,256]{2,1,0:T(8,128)(2,1)S(1)} %copy-done.4), custom_call_target="tpu_custom_call" | custom-call | flops 805306368 | bytes 8388608 | tf_op jit(solution)/shard_map/pallas_call | solution.py:230
  112.2 6.5 %shard_map.97 = (bf16[8,512,384]{2,1,0:T(8,128)(2,1)}, bf16[8,512,384]{2,1,0:T(8,128)(2,1)}) custom-call(bf16[32,2,8,16,384]{4,3,2,1,0:T(8,128)(2,1)S(1)} %all_to_all.5.b_ref.g_ref, bf16[8,512,512]{2,1,0:T(8,128)(2,1)S(1)} %copy-done.3, bf16[8,512,384]{2,1,0:T(8,128)(2,1)S(1)} %copy-done, bf16[8,512,384]{2,1,0:T(8,128)(2,1)S(1)} %copy-done.1), custom_call_target="tpu_custom_call" | custom-call | flops 3221225472 | bytes 19922944 | tf_op jit(solution)/shard_map/pallas_call | solution.py:173
  118.7 24.8 %collective-permute-done.3 = bf16[4,256,256]{2,1,0:T(8,128)(2,1)S(1)} collective-permute-done((bf16[4,256,256]{2,1,0:T(8,128)(2,1)S(1)}, bf16[4,256,256]{2,1,0:T(8,128)(2,1)S(1)}, u32[]{:S(2)}, u32[]{:S(2)}) %collective-permute-start.3) | collective-permute-done | bytes 524320 | tf_op jit(solution)/shard_map/ppermute | solution.py:245
  143.5 1.0 fusion.2
  144.5 0.0 collective-permute-done.2
  144.5 1.4 fusion
  (6 shorter events, 0.0 us)
Async XLA Ops:
  10.3 84.5 %copy-start = (bf16[8,512,384]{2,1,0:T(8,128)(2,1)S(1)}, bf16[8,512,384]{2,1,0:T(8,128)(2,1)}, u32[]{:S(2)}) copy-start(bf16[8,512,384]{2,1,0:T(8,128)(2,1)} %t_ref.3) | copy-start | bytes 9437188
  10.3 84.5 %copy-start.1 = (bf16[8,512,384]{2,1,0:T(8,128)(2,1)S(1)}, bf16[8,512,384]{2,1,0:T(8,128)(2,1)}, u32[]{:S(2)}) copy-start(bf16[8,512,384]{2,1,0:T(8,128)(2,1)} %g_ref.2) | copy-start | bytes 9437188
  94.8 7.2 %copy-start.2 = (bf16[16,256,384]{2,1,0:T(8,128)(2,1)S(1)}, bf16[16,256,384]{2,1,0:T(8,128)(2,1)}, u32[]{:S(2)}) copy-start(bf16[16,256,384]{2,1,0:T(8,128)(2,1)} %c_ref.3) | copy-start | bytes 9437188
  100.1 7.4 %collective-permute-start = (bf16[2,8,128,512]{3,2,1,0:T(8,128)(2,1)S(1)}, bf16[2,8,128,512]{3,2,1,0:T(8,128)(2,1)S(1)}, u32[]{:S(2)}, u32[]{:S(2)}) collective-permute-start(bf16[2,8,128,512]{3,2,1,0:T(8,128)(2,1)S(1)} %get-tuple-element.18), channel_id=1, source_target_pairs={{0,1},{1,0},{2,3},{3,2},{4,5},{5,4},{6,7},{7,6},{8,9},{9,8},{10,11... | collective-permute-start | bytes 6291464 | tf_op jit(solution)/shard_map/ppermute | solution.py:245
  103.7 3.6 %collective-permute-start.1 = (bf16[2,4,256,256]{3,2,1,0:T(8,128)(2,1)S(1)}, bf16[2,4,256,256]{3,2,1,0:T(8,128)(2,1)S(1)}, u32[]{:S(2)}, u32[]{:S(2)}) collective-permute-start(bf16[2,4,256,256]{3,2,1,0:T(8,128)(2,1)S(1)} %shard_map.95), channel_id=1, source_target_pairs={{0,1},{1,0},{2,3},{3,2},{4,5},{5,4},{6,7},{7,6},{8,9},{9,8},{10,11... | collective-permute-start | bytes 3145736 | tf_op jit(solution)/shard_map/ppermute | solution.py:245
  105.5 3.8 %copy-start.4 = (bf16[16,256,256]{2,1,0:T(8,128)(2,1)S(1)}, bf16[16,256,256]{2,1,0:T(8,128)(2,1)}, u32[]{:S(2)}) copy-start(bf16[16,256,256]{2,1,0:T(8,128)(2,1)} %s_ref) | copy-start | bytes 6291460
  107.8 36.7 %collective-permute-start.2 = (bf16[8,128,512]{2,1,0:T(8,128)(2,1)S(1)}, bf16[8,128,512]{2,1,0:T(8,128)(2,1)S(1)}, u32[]{:S(2)}, u32[]{:S(2)}) collective-permute-start(bf16[8,128,512]{2,1,0:T(8,128)(2,1)S(1)} %fusion.1), channel_id=1, source_target_pairs={{0,2},{1,3},{2,0},{3,1},{4,6},{5,7},{6,4},{7,5},{8,10},{9,11},{10,... | collective-permute-start | bytes 3145736 | tf_op jit(solution)/shard_map/ppermute | solution.py:245
  108.2 35.3 %collective-permute-start.3 = (bf16[4,256,256]{2,1,0:T(8,128)(2,1)S(1)}, bf16[4,256,256]{2,1,0:T(8,128)(2,1)S(1)}, u32[]{:S(2)}, u32[]{:S(2)}) collective-permute-start(bf16[4,256,256]{2,1,0:T(8,128)(2,1)S(1)} %fusion.3), channel_id=1, source_target_pairs={{0,2},{1,3},{2,0},{3,1},{4,6},{5,7},{6,4},{7,5},{8,10},{9,11},{10,... | collective-permute-start | bytes 1572872 | tf_op jit(solution)/shard_map/ppermute | solution.py:245
  109.3 2.9 %copy-start.3 = (bf16[8,512,512]{2,1,0:T(8,128)(2,1)S(1)}, bf16[8,512,512]{2,1,0:T(8,128)(2,1)}, u32[]{:S(2)}) copy-start(bf16[8,512,512]{2,1,0:T(8,128)(2,1)} %f_ref.1) | copy-start | bytes 12582916

commit v3 on v2

v3 whole, which is shorter than its diff:
```python
import jax
import jax.numpy as jnp
from jax import lax
from jax.experimental import pallas as pl
from jax.experimental.pallas import tpu as pltpu
from jax.sharding import PartitionSpec as P

F32 = jnp.float32
BF16 = jnp.bfloat16
MIB = 1024 * 1024
LANES = 128
PAD = 1
SCALE = 100000

NN = (((1,), (0,)), ((), ()))
NT = (((1,), (1,)), ((), ()))
TN = (((0,), (0,)), ((), ()))

HERE, ACROSS, BESIDE, OPPOSITE = range(4)

GRAD, GATED = range(2)


def dot(a, b, dims):
    return lax.dot_general(a, b, dims, preferred_element_type=F32)


def params(mib=60):
    return pltpu.CompilerParams(vmem_limit_bytes=mib * MIB)


def cost(flops, nbytes):
    return pl.CostEstimate(flops=flops // SCALE, bytes_accessed=nbytes // SCALE, transcendentals=0)


def lanes(t):
    return slice(t * LANES, (t + 1) * LANES)


def send_slabs(second_blocks, cotangent, first_blocks, tokens, gate_values, devices):
    cols, all_rows, d = cotangent.shape
    rows, all_cols, _ = tokens.shape
    tiles, pairs = d // LANES, cols // 2
    chunk, span = 4, 128
    chunks, spans = cols // chunk, all_cols // span
    back_pitch, gated_pitch = all_rows + PAD, span + PAD

    def kernel(s_hbm, c_hbm, f_hbm, t_hbm, g_hbm, out_ref, s_ref, c_ref, f_ref, t_ref, g_ref, back, gated, sems):
        fetches = []

        def fetch(at, *sources_and_targets):
            for source, target in sources_and_targets:
                copy = pltpu.make_async_copy(source.at[at], target.at[at], sems.at[len(fetches)])
                copy.start()
                fetches.append(copy)

        def arrive(first, count):
            for copy in fetches[first:first + count]:
                copy.wait()

        for i in range(chunks):
            fetch(pl.ds(i * chunk, chunk), (s_hbm, s_ref), (c_hbm, c_ref))
        fetch(pl.ds(0, rows), (t_hbm, t_ref))
        for i in range(spans):
            fetch((pl.ds(0, rows), pl.ds(i * span, span)), (f_hbm, f_ref), (g_hbm, g_ref))

        for i in range(chunks):
            arrive(2 * i, 2)
            for c in range(i * chunk, (i + 1) * chunk):
                product = dot(s_ref[c], c_ref[c], TN)
                for t in range(tiles):
                    back[t, c * back_pitch:c * back_pitch + all_rows, :] = product[:, lanes(t)]

        def rows_of(k, carry):
            for r in range(rows):
                for t in range(tiles):
                    strip = back[t, pl.ds(k * rows + r, cols, stride=back_pitch), :]
                    out_ref[k, GRAD, r, :, lanes(t)] = strip.astype(BF16)
            return carry

        lax.fori_loop(0, devices, rows_of, 0, unroll=2)

        arrive(2 * chunks, 1)
        for i in range(spans):
            arrive(2 * chunks + 1 + 2 * i, 2)
            part = pl.ds(i * span, span)
            for r in range(rows):
                product = dot(f_ref[r, part, :], t_ref[r], NN) * g_ref[r, part, :].astype(F32)
                for t in range(tiles):
                    gated[t, r * gated_pitch:r * gated_pitch + span, :] = product[:, lanes(t)]

            def columns_of(k, carry):
                for j in range(pairs):
                    at = k * cols + 2 * j
                    for t in range(tiles):
                        even = gated[t, pl.ds(at, rows, stride=gated_pitch), :]
                        odd = gated[t, pl.ds(at + 1, rows, stride=gated_pitch), :]
                        pair = jnp.concatenate([even, odd], axis=0)
                        out_ref[i * (span // cols) + k, GATED, j, :, lanes(t)] = pair.astype(BF16)
                return carry

            lax.fori_loop(0, span // cols, columns_of, 0, unroll=2)

    hbm = pl.BlockSpec(memory_space=pltpu.HBM)
    return pl.pallas_call(
        kernel,
        in_specs=[hbm] * 5,
        out_specs=pl.BlockSpec(memory_space=pltpu.VMEM),
        out_shape=pltpu.VMEM((devices, 2, rows, cols, d), BF16),
        scratch_shapes=[
            pltpu.VMEM(second_blocks.shape, BF16),
            pltpu.VMEM(cotangent.shape, BF16),
            pltpu.VMEM(first_blocks.shape, BF16),
            pltpu.VMEM(tokens.shape, BF16),
            pltpu.VMEM(gate_values.shape, BF16),
            pltpu.VMEM((tiles, (cols + 1) * back_pitch + 7, LANES), F32),
            pltpu.VMEM((tiles, (rows + 1) * gated_pitch + 7, LANES), F32),
            pltpu.SemaphoreType.DMA((2 * chunks + 1 + 2 * spans,)),
        ],
        compiler_params=params(48),
        cost_estimate=cost(
            2 * cols * all_rows * all_rows * d + 2 * rows * all_cols * all_cols * d,
            2 * cols * all_rows * (all_rows + 2 * d) + 2 * rows * all_cols * (all_cols + 3 * d),
        ),
    )(second_blocks, cotangent, first_blocks, tokens, gate_values)


def grad_spec(slabs, step):
    devices, _, _, both, d = slabs.shape
    return pl.BlockSpec((devices, 1, step, both, d), lambda i: (0, GRAD, i, 0, 0))


def first_terms(place, whose, slabs, tokens, gate_values):
    rows, cols, d = tokens.shape
    part, step = cols // 4, 4

    def kernel(place_ref, b_ref, t_ref, g_ref, out_ref):
        for r in range(step):
            back = b_ref[:, 0, r].reshape(part, d).astype(F32)
            hidden_grad = (back * g_ref[r].astype(F32)).astype(BF16)
            out_ref[r] = dot(hidden_grad, t_ref[r], NT).astype(BF16)

    devices, _, _, both, _ = slabs.shape
    return pl.pallas_call(
        kernel,
        grid_spec=pltpu.PrefetchScalarGridSpec(
            num_scalar_prefetch=1,
            grid=(rows // step,),
            in_specs=[
                pl.BlockSpec((devices // 4, 1, step, both, d), lambda i, at: (at[whose], GRAD, i, 0, 0)),
                pl.BlockSpec((step, cols, d), lambda i, at: (i, 0, 0)),
                pl.BlockSpec((step, part, d), lambda i, at: (i, at[whose], 0)),
            ],
            out_specs=pl.BlockSpec((step, part, cols), lambda i, at: (i, 0, 0)),
        ),
        out_shape=jax.ShapeDtypeStruct((rows, part, cols), BF16),
        compiler_params=params(24),
        cost_estimate=cost(rows * cols * part * d * 2, 2 * rows * (cols * part + 2 * part * d + cols * d)),
    )(place, slabs, tokens, gate_values)


def row_grads(slabs, first_blocks, tokens, gate_values):
    rows, cols, d = tokens.shape

    step = 2

    def kernel(b_ref, f_ref, t_ref, g_ref, tg_ref, gg_ref):
        for k in range(step):
            back = b_ref[:, 0, k].reshape(cols, d).astype(F32)
            hidden_grad = (back * g_ref[k].astype(F32)).astype(BF16)
            tg_ref[k] = dot(f_ref[k], hidden_grad, TN).astype(BF16)
            gg_ref[k] = (back * dot(f_ref[k], t_ref[k], NN)).astype(BF16)

    row_spec = pl.BlockSpec((step, cols, d), lambda i: (i, 0, 0))
    row_shape = jax.ShapeDtypeStruct((rows, cols, d), BF16)
    return pl.pallas_call(
        kernel,
        grid=(rows // step,),
        in_specs=[grad_spec(slabs, step), pl.BlockSpec((step, cols, cols), lambda i: (i, 0, 0)), row_spec, row_spec],
        out_specs=[row_spec, row_spec],
        out_shape=[row_shape, row_shape],
        compiler_params=params(24),
        cost_estimate=cost(4 * rows * cols * cols * d, 2 * rows * cols * (cols + 5 * d)),
    )(slabs, first_blocks, tokens, gate_values)


def column_pair(g_ref, k):
    devices, _, _, both, d = g_ref.shape
    pair = g_ref[:, 0, k].astype(F32).reshape(devices, 2, both // 2, d)
    return [pair[:, c].reshape(devices * both // 2, d).astype(BF16) for c in range(2)]


def second_terms(place, whose, slabs, cotangent):
    cols, rows, d = cotangent.shape
    devices, _, pairs, both, _ = slabs.shape
    step, part = pairs // 4, cols // 4

    def kernel(place_ref, g_ref, c_ref, out_ref):
        for k in range(step):
            for c, column in enumerate(column_pair(g_ref, k)):
                out_ref[2 * k + c] = dot(c_ref[2 * k + c], column, NT).astype(BF16)

    return pl.pallas_call(
        kernel,
        grid_spec=pltpu.PrefetchScalarGridSpec(
            num_scalar_prefetch=1,
            grid=(1,),
            in_specs=[
                pl.BlockSpec((devices, 1, step, both, d), lambda i, at: (0, GATED, at[whose], 0, 0)),
                pl.BlockSpec((part, rows, d), lambda i, at: (at[whose], 0, 0)),
            ],
            out_specs=pl.BlockSpec((part, rows, rows), lambda i, at: (0, 0, 0)),
        ),
        out_shape=jax.ShapeDtypeStruct((part, rows, rows), BF16),
        compiler_params=params(24),
        cost_estimate=cost(2 * part * rows * rows * d, 2 * part * rows * (rows + 2 * d)),
    )(place, slabs, cotangent)


def mixed_columns(slabs, second_blocks):
    cols, rows, _ = second_blocks.shape
    devices, _, pairs, both, d = slabs.shape
    step = 4

    def kernel(g_ref, s_ref, out_ref):
        for k in range(step):
            for c, column in enumerate(column_pair(g_ref, k)):
                out_ref[2 * k + c] = dot(s_ref[2 * k + c], column, NN).astype(BF16)

    return pl.pallas_call(
        kernel,
        grid=(pairs // step,),
        in_specs=[
            pl.BlockSpec((devices, 1, step, both, d), lambda i: (0, GATED, i, 0, 0)),
            pl.BlockSpec((2 * step, rows, rows), lambda i: (i, 0, 0)),
        ],
        out_specs=pl.BlockSpec((2 * step, rows, d), lambda i: (i, 0, 0)),
        out_shape=jax.ShapeDtypeStruct((cols, rows, d), BF16),
        compiler_params=params(24),
        cost_estimate=cost(2 * cols * rows * rows * d, 2 * cols * rows * (rows + 2 * d)),
    )(slabs, second_blocks)


def swap(x, bit):
    return lax.ppermute(x, "ch", [(i, i ^ bit) for i in range(4)])


def add(a, b):
    return a.astype(F32) + b.astype(F32)


def after(first, *later):
    return lax.optimization_barrier((first, *later))


def local(tokens, gate_values, first_blocks, second_blocks, cotangent):
    ch = lax.axis_index("ch")
    place = jnp.stack([ch, ch ^ 2, ch ^ 1, ch ^ 3]).astype(jnp.int32)

    slabs = send_slabs(second_blocks, cotangent, first_blocks, tokens, gate_values, lax.axis_size("seq"))
    slabs, place = after(slabs, place)
    slabs = lax.all_to_all(slabs, "seq", split_axis=0, concat_axis=0, tiled=True)

    def terms(whose):
        return first_terms(place, whose, slabs, tokens, gate_values), second_terms(place, whose, slabs, cotangent)

    def over_cores(whose, whose_beside):
        first, second = terms(whose_beside)
        first, second = swap(first, 1), swap(second, 1)
        near_first, near_second = terms(whose)
        return add(near_first, first), add(near_second, second)

    away = [x.astype(BF16) for x in over_cores(ACROSS, OPPOSITE)]
    *away, second_blocks = after(*away, second_blocks)
    across_c, across_b = swap(away[1], 2), swap(away[0], 2)
    mixed_output = mixed_columns(slabs, second_blocks)
    across_c, mixed_output, tokens, gate_values, cotangent = after(
        across_c, mixed_output, tokens, gate_values, cotangent
    )
    here_b, here_c = over_cores(HERE, BESIDE)
    second_grad, gate_values = after((here_c + across_c.astype(F32)).astype(BF16), gate_values)
    token_grad, gate_grad = row_grads(slabs, first_blocks, tokens, gate_values)
    first_grad = (here_b + across_b.astype(F32)).astype(BF16)
    return (mixed_output, token_grad, gate_grad, first_grad, second_grad)


def solution(mesh):
    return jax.shard_map(
        local,
        mesh=mesh,
        in_specs=(
            P("seq", None, "ch"),
            P("seq", None, "ch"),
            P("seq", None, None),
            P("seq", None, None),
            P("seq", None, "ch"),
        ),
        out_specs=(
            P("seq", None, "ch"),
            P("seq", None, "ch"),
            P("seq", None, "ch"),
            P("seq", "ch", None),
            P(("seq", "ch"), None, None),
        ),
        check_vma=False,
    )
```

time: 146 us -> 139 us (0.952)
  waiting for transfers between devices: 26.5 us -> 14.7 us
  starting transfers between devices: 3.6 us -> 6.28 us
  Pallas kernels: 27.5 us -> 29.2 us
    ppermute x4 -> x6, waiting for transfers between devices: 26.5 us -> 14.7 us  [swap(): return lax.ppermute(x, 'ch', [(i, i ^ bit) for i in range(4)])]
    pallas_call x2 -> x5, Pallas kernels: 11.7 us -> 14.7 us  [the longest x4 8.27 us: first_terms(): pl.pallas_call(kernel, grid_spec=pltpu.PrefetchScalarGridSpec(num_scalar_...]
    ppermute x4 -> x6, starting transfers between devices: 3.6 us -> 6.28 us  [swap(): return lax.ppermute(x, 'ch', [(i, i ^ bit) for i in range(4)])]
    pallas_call x1, Pallas kernels: 9.57 us -> 7.5 us  [send_slabs(): pl.pallas_call(kernel, in_specs=[hbm] * 5, out_specs=pl.BlockSpec(memory_...]
    pallas_call x2 -> x4, Pallas kernels: 3.41 us -> 4.05 us  [second_terms(): pl.pallas_call(kernel, grid_spec=pltpu.PrefetchScalarGridSpec(num_scalar_...]
  transfers between devices with their start and end apart: 4 -> 6, of which waited for: 2 -> 2; matrix products, arithmetic and copies ran while one was open for 1% -> 1% of each run, Pallas kernels for 9% -> 14%
where the time goes in v3:
time: 139 us; the launch traced here: 138 us
  blocking collectives  84.5 us (61%)
  Pallas kernels  29.2 us (21%)
  waiting for transfers between devices  14.7 us (11%)
  starting transfers between devices  6.28 us (5%)
  other arithmetic  2.98 us (2%)
    all_to_all x1, blocking collectives, local(): lax.all_to_all(slabs, 'seq', split_axis=0, concat_axis=0, tiled=True)  84.5 us
    ppermute x6, waiting for transfers between devices, swap(): return lax.ppermute(x, 'ch', [(i, i ^ bit) for i in range(4)])  14.7 us
    pallas_call x4, Pallas kernels, first_terms(): pl.pallas_call(kernel, grid_spec=pltpu.PrefetchScalarGridSpec(num_scalar_...  8.27 us
    pallas_call x1, Pallas kernels, send_slabs(): pl.pallas_call(kernel, in_specs=[hbm] * 5, out_specs=pl.BlockSpec(memory_...  7.5 us
    pallas_call x1, Pallas kernels, row_grads(): pl.pallas_call(kernel, grid=(rows // step,), in_specs=[grad_spec(slabs, s...  6.45 us
    ppermute x6, starting transfers between devices, swap(): return lax.ppermute(x, 'ch', [(i, i ^ bit) for i in range(4)])  6.28 us
    pallas_call x4, Pallas kernels, second_terms(): pl.pallas_call(kernel, grid_spec=pltpu.PrefetchScalarGridSpec(num_scalar_...  4.05 us
    pallas_call x1, Pallas kernels, mixed_columns(): pl.pallas_call(kernel, grid=(pairs // step,), in_specs=[pl.BlockSpec((dev...  2.89 us
  transfers between devices with their start and end apart: 6, of which 2 were waited for; matrix products, arithmetic and copies ran while one was open for 1% of the time, Pallas kernels for 14%

profile of v3, /device:TPU:1, one launch (start us, length us, event | category | flops | bytes accessed | tf_op | source)
XLA Modules:
  0.0 138.5 jit_solution(7916188175282955207)
XLA Ops:
  0.7 7.5 %shard_map.92 = bf16[32,2,8,16,384]{4,3,2,1,0:T(8,128)(2,1)S(1)} custom-call(bf16[16,256,256]{2,1,0:T(8,128)(2,1)} %s_ref, bf16[16,256,384]{2,1,0:T(8,128)(2,1)} %c_ref.5, bf16[8,512,512]{2,1,0:T(8,128)(2,1)} %f_ref.1, bf16[8,512,384]{2,1,0:T(8,128)(2,1)} %t_ref.6, bf16[8,512,384]{2,1,0:T(8,128)(2,1)} %g_ref.6), custom_call_target="tpu_custom_call" | custom-call | flops 24159 | bytes 220 | tf_op jit(solution)/shard_map/pallas_call | solution.py:105
  8.2 84.5 %all_to_all.5.b_ref.g_ref = bf16[32,2,8,16,384]{4,3,2,1,0:T(8,128)(2,1)S(1)} all-to-all(bf16[32,2,8,16,384]{4,3,2,1,0:T(8,128)(2,1)S(1)} %shard_map.92), channel_id=1, replica_groups=mesh['seq'=32,'ch'=4] {'seq'}, dimensions={0} | all-to-all | bytes 12582912 | tf_op jit(solution)/shard_map/all_to_all | solution.py:262
  92.8 2.1 %shard_map.94 = bf16[8,128,512]{2,1,0:T(8,128)(2,1)S(1)} custom-call(s32[4]{0:T(128)S(1)} %pad_add_fusion.place_ref, bf16[32,2,8,16,384]{4,3,2,1,0:T(8,128)(2,1)S(1)} %all_to_all.5.b_ref.g_ref, bf16[8,512,384]{2,1,0:T(8,128)(2,1)S(1)} %copy-done, bf16[8,512,384]{2,1,0:T(8,128)(2,1)S(1)} %copy-done.1), custom_call_target="tpu_custom_call" | custom-call | flops 4026 | bytes 57 | tf_op jit(solution)/shard_map/pallas_call | solution.py:144
  94.8 1.9 %collective-permute-start = (bf16[8,128,512]{2,1,0:T(8,128)(2,1)S(1)}, bf16[8,128,512]{2,1,0:T(8,128)(2,1)S(1)}, u32[]{:S(2)}, u32[]{:S(2)}) collective-permute-start(bf16[8,128,512]{2,1,0:T(8,128)(2,1)S(1)} %shard_map.94), channel_id=1, source_target_pairs={{0,1},{1,0},{2,3},{3,2},{4,5},{5,4},{6,7},{7,6},{8,9},{9,8},{10,11... | collective-permute-start | bytes 3145736 | tf_op jit(solution)/shard_map/ppermute | solution.py:245
  96.8 1.0 shard_map.96
  97.8 0.1 collective-permute-start.1
  97.9 1.0 shard_map.95
  98.9 2.1 %shard_map.93 = bf16[8,128,512]{2,1,0:T(8,128)(2,1)S(1)} custom-call(s32[4]{0:T(128)S(1)} %pad_add_fusion.place_ref, bf16[32,2,8,16,384]{4,3,2,1,0:T(8,128)(2,1)S(1)} %all_to_all.5.b_ref.g_ref, bf16[8,512,384]{2,1,0:T(8,128)(2,1)S(1)} %copy-done, bf16[8,512,384]{2,1,0:T(8,128)(2,1)S(1)} %copy-done.1), custom_call_target="tpu_custom_call" | custom-call | flops 4026 | bytes 57 | tf_op jit(solution)/shard_map/pallas_call | solution.py:144
  101.0 0.1 add_convert_fusion.3
  101.2 0.3 add_convert_fusion.1
  101.5 0.4 collective-permute-start.2
  101.9 1.1 collective-permute-start.5
  103.0 2.9 %shard_map.97 = bf16[16,256,384]{2,1,0:T(8,128)(2,1)} custom-call(bf16[32,2,8,16,384]{4,3,2,1,0:T(8,128)(2,1)S(1)} %all_to_all.5.b_ref.g_ref, bf16[16,256,256]{2,1,0:T(8,128)(2,1)S(1)} %copy-done.4), custom_call_target="tpu_custom_call" | custom-call | flops 8053 | bytes 83 | tf_op jit(solution)/shard_map/pallas_call | solution.py:230
  105.9 8.6 %collective-permute-done.2 = bf16[4,256,256]{2,1,0:T(8,128)(2,1)S(1)} collective-permute-done((bf16[4,256,256]{2,1,0:T(8,128)(2,1)S(1)}, bf16[4,256,256]{2,1,0:T(8,128)(2,1)S(1)}, u32[]{:S(2)}, u32[]{:S(2)}) %collective-permute-start.2) | collective-permute-done | bytes 524320 | tf_op jit(solution)/shard_map/ppermute | solution.py:245
  114.5 2.1 %shard_map.102 = bf16[8,128,512]{2,1,0:T(8,128)(2,1)S(1)} custom-call(s32[4]{0:T(128)S(1)} %pad_add_fusion.place_ref, bf16[32,2,8,16,384]{4,3,2,1,0:T(8,128)(2,1)S(1)} %all_to_all.5.b_ref.g_ref, bf16[8,512,384]{2,1,0:T(8,128)(2,1)S(1)} %copy-done, bf16[8,512,384]{2,1,0:T(8,128)(2,1)S(1)} %copy-done.1), custom_call_target="tpu_custom_call" | custom-call | flops 4026 | bytes 57 | tf_op jit(solution)/shard_map/pallas_call | solution.py:144
  116.6 2.4 %collective-permute-start.4 = (bf16[8,128,512]{2,1,0:T(8,128)(2,1)S(1)}, bf16[8,128,512]{2,1,0:T(8,128)(2,1)S(1)}, u32[]{:S(2)}, u32[]{:S(2)}) collective-permute-start(bf16[8,128,512]{2,1,0:T(8,128)(2,1)S(1)} %shard_map.102), channel_id=1, source_target_pairs={{0,1},{1,0},{2,3},{3,2},{4,5},{5,4},{6,7},{7,6},{8,9},{9,8},{10,11... | collective-permute-start | bytes 3145736 | tf_op jit(solution)/shard_map/ppermute | solution.py:245
  119.0 1.0 shard_map.99
  120.0 0.3 collective-permute-start.3
  120.3 1.0 shard_map.98
  121.4 2.1 %shard_map.101 = bf16[8,128,512]{2,1,0:T(8,128)(2,1)S(1)} custom-call(s32[4]{0:T(128)S(1)} %pad_add_fusion.place_ref, bf16[32,2,8,16,384]{4,3,2,1,0:T(8,128)(2,1)S(1)} %all_to_all.5.b_ref.g_ref, bf16[8,512,384]{2,1,0:T(8,128)(2,1)S(1)} %copy-done, bf16[8,512,384]{2,1,0:T(8,128)(2,1)S(1)} %copy-done.1), custom_call_target="tpu_custom_call" | custom-call | flops 4026 | bytes 57 | tf_op jit(solution)/shard_map/pallas_call | solution.py:144
  123.4 1.0 add_convert_fusion.2
  124.5 6.4 %shard_map.100 = (bf16[8,512,384]{2,1,0:T(8,128)(2,1)}, bf16[8,512,384]{2,1,0:T(8,128)(2,1)}) custom-call(bf16[32,2,8,16,384]{4,3,2,1,0:T(8,128)(2,1)S(1)} %all_to_all.5.b_ref.g_ref, bf16[8,512,512]{2,1,0:T(8,128)(2,1)S(1)} %copy-done.3, bf16[8,512,384]{2,1,0:T(8,128)(2,1)S(1)} %copy-done, bf16[8,512,384]{2,1,0:T(8,128)(2,1)S(1)} %copy-done.1), custom_call_target="tpu_custom_call" | custom-call | flops 32212 | bytes 199 | tf_op jit(solution)/shard_map/pallas_call | solution.py:176
  130.9 6.1 %collective-permute-done.5 = bf16[8,128,512]{2,1,0:T(8,128)(2,1)S(1)} collective-permute-done((bf16[8,128,512]{2,1,0:T(8,128)(2,1)S(1)}, bf16[8,128,512]{2,1,0:T(8,128)(2,1)S(1)}, u32[]{:S(2)}, u32[]{:S(2)}) %collective-permute-start.5) | collective-permute-done | bytes 1048608 | tf_op jit(solution)/shard_map/ppermute | solution.py:245
  137.0 1.5 %add_convert_fusion = bf16[8,128,512]{2,1,0:T(8,128)(2,1)} fusion(bf16[8,128,512]{2,1,0:T(8,128)(2,1)S(1)} %collective-permute-done.5, bf16[8,128,512]{2,1,0:T(8,128)(2,1)S(1)} %collective-permute-done.4, bf16[8,128,512]{2,1,0:T(8,128)(2,1)S(1)} %shard_map.101), kind=kLoop, calls=%fused_computation | loop fusion | flops 3145728 | bytes 4194304 | tf_op jit(solution)/shard_map/convert_element_type | solution.py:283
  (15 shorter events, 0.1 us)
Async XLA Ops:
  8.2 84.5 %copy-start = (bf16[8,512,384]{2,1,0:T(8,128)(2,1)S(1)}, bf16[8,512,384]{2,1,0:T(8,128)(2,1)}, u32[]{:S(2)}) copy-start(bf16[8,512,384]{2,1,0:T(8,128)(2,1)} %t_ref.6) | copy-start | bytes 9437188
  8.2 84.5 %copy-start.1 = (bf16[8,512,384]{2,1,0:T(8,128)(2,1)S(1)}, bf16[8,512,384]{2,1,0:T(8,128)(2,1)}, u32[]{:S(2)}) copy-start(bf16[8,512,384]{2,1,0:T(8,128)(2,1)} %g_ref.6) | copy-start | bytes 9437188
  92.8 4.0 %copy-start.2 = (bf16[16,256,384]{2,1,0:T(8,128)(2,1)S(1)}, bf16[16,256,384]{2,1,0:T(8,128)(2,1)}, u32[]{:S(2)}) copy-start(bf16[16,256,384]{2,1,0:T(8,128)(2,1)} %c_ref.5) | copy-start | bytes 9437188
  94.8 6.3 %collective-permute-start = (bf16[8,128,512]{2,1,0:T(8,128)(2,1)S(1)}, bf16[8,128,512]{2,1,0:T(8,128)(2,1)S(1)}, u32[]{:S(2)}, u32[]{:S(2)}) collective-permute-start(bf16[8,128,512]{2,1,0:T(8,128)(2,1)S(1)} %shard_map.94), channel_id=1, source_target_pairs={{0,1},{1,0},{2,3},{3,2},{4,5},{5,4},{6,7},{7,6},{8,9},{9,8},{10,11... | collective-permute-start | bytes 3145736 | tf_op jit(solution)/shard_map/ppermute | solution.py:245
  97.8 3.2 %collective-permute-start.1 = (bf16[4,256,256]{2,1,0:T(8,128)(2,1)S(1)}, bf16[4,256,256]{2,1,0:T(8,128)(2,1)S(1)}, u32[]{:S(2)}, u32[]{:S(2)}) collective-permute-start(bf16[4,256,256]{2,1,0:T(8,128)(2,1)S(1)} %shard_map.96), channel_id=1, source_target_pairs={{0,1},{1,0},{2,3},{3,2},{4,5},{5,4},{6,7},{7,6},{8,9},{9,8},{10,11... | collective-permute-start | bytes 1572872 | tf_op jit(solution)/shard_map/ppermute | solution.py:245
  101.0 2.0 %copy-start.4 = (bf16[16,256,256]{2,1,0:T(8,128)(2,1)S(1)}, bf16[16,256,256]{2,1,0:T(8,128)(2,1)}, u32[]{:S(2)}) copy-start(bf16[16,256,256]{2,1,0:T(8,128)(2,1)} %s_ref) | copy-start | bytes 6291460
  101.5 13.1 %collective-permute-start.2 = (bf16[4,256,256]{2,1,0:T(8,128)(2,1)S(1)}, bf16[4,256,256]{2,1,0:T(8,128)(2,1)S(1)}, u32[]{:S(2)}, u32[]{:S(2)}) collective-permute-start(bf16[4,256,256]{2,1,0:T(8,128)(2,1)S(1)} %add_convert_fusion.3), channel_id=1, source_target_pairs={{0,2},{1,3},{2,0},{3,1},{4,6},{5,7},{6,4},{7,5},{8,10},{9,11},{10,... | collective-permute-start | bytes 1572872 | tf_op jit(solution)/shard_map/ppermute | solution.py:245
  101.9 35.1 %collective-permute-start.5 = (bf16[8,128,512]{2,1,0:T(8,128)(2,1)S(1)}, bf16[8,128,512]{2,1,0:T(8,128)(2,1)S(1)}, u32[]{:S(2)}, u32[]{:S(2)}) collective-permute-start(bf16[8,128,512]{2,1,0:T(8,128)(2,1)S(1)} %add_convert_fusion.1), channel_id=1, source_target_pairs={{0,2},{1,3},{2,0},{3,1},{4,6},{5,7},{6,4},{7,5},{8,10},{9,11},{10,... | collective-permute-start | bytes 3145736 | tf_op jit(solution)/shard_map/ppermute | solution.py:245
  116.6 20.4 %collective-permute-start.4 = (bf16[8,128,512]{2,1,0:T(8,128)(2,1)S(1)}, bf16[8,128,512]{2,1,0:T(8,128)(2,1)S(1)}, u32[]{:S(2)}, u32[]{:S(2)}) collective-permute-start(bf16[8,128,512]{2,1,0:T(8,128)(2,1)S(1)} %shard_map.102), channel_id=1, source_target_pairs={{0,1},{1,0},{2,3},{3,2},{4,5},{5,4},{6,7},{7,6},{8,9},{9,8},{10,11... | collective-permute-start | bytes 3145736 | tf_op jit(solution)/shard_map/ppermute | solution.py:245
  120.0 3.4 %collective-permute-start.3 = (bf16[4,256,256]{2,1,0:T(8,128)(2,1)S(1)}, bf16[4,256,256]{2,1,0:T(8,128)(2,1)S(1)}, u32[]{:S(2)}, u32[]{:S(2)}) collective-permute-start(bf16[4,256,256]{2,1,0:T(8,128)(2,1)S(1)} %shard_map.99), channel_id=1, source_target_pairs={{0,1},{1,0},{2,3},{3,2},{4,5},{5,4},{6,7},{7,6},{8,9},{9,8},{10,11... | collective-permute-start | bytes 1572872 | tf_op jit(solution)/shard_map/ppermute | solution.py:245
  121.3 3.1 %copy-start.3 = (bf16[8,512,512]{2,1,0:T(8,128)(2,1)S(1)}, bf16[8,512,512]{2,1,0:T(8,128)(2,1)}, u32[]{:S(2)}) copy-start(bf16[8,512,512]{2,1,0:T(8,128)(2,1)} %f_ref.1) | copy-start | bytes 12582916

commit v4 on v3

--- a/solution.py
+++ b/solution.py
@@ -132,30 +132,30 @@
 
 def first_terms(place, whose, slabs, tokens, gate_values):
     rows, cols, d = tokens.shape
-    part, step = cols // 4, 4
-
-    def kernel(place_ref, b_ref, t_ref, g_ref, out_ref):
-        for r in range(step):
-            back = b_ref[:, 0, r].reshape(part, d).astype(F32)
-            hidden_grad = (back * g_ref[r].astype(F32)).astype(BF16)
-            out_ref[r] = dot(hidden_grad, t_ref[r], NT).astype(BF16)
-
-    devices, _, _, both, _ = slabs.shape
-    return pl.pallas_call(
-        kernel,
-        grid_spec=pltpu.PrefetchScalarGridSpec(
-            num_scalar_prefetch=1,
-            grid=(rows // step,),
-            in_specs=[
-                pl.BlockSpec((devices // 4, 1, step, both, d), lambda i, at: (at[whose], GRAD, i, 0, 0)),
-                pl.BlockSpec((step, cols, d), lambda i, at: (i, 0, 0)),
-                pl.BlockSpec((step, part, d), lambda i, at: (i, at[whose], 0)),
-            ],
-            out_specs=pl.BlockSpec((step, part, cols), lambda i, at: (i, 0, 0)),
-        ),
-        out_shape=jax.ShapeDtypeStruct((rows, part, cols), BF16),
-        compiler_params=params(24),
-        cost_estimate=cost(rows * cols * part * d * 2, 2 * rows * (cols * part + 2 * part * d + cols * d)),
+    devices, part = slabs.shape[0], cols // 4
+    group, count = devices // 4, len(whose)
+
+    def kernel(place_ref, b_ref, t_ref, g_ref, *rest):
+        outs, held = rest[:count], rest[count]
+        for r in range(rows):
+            for k, name in enumerate(whose):
+                at = place_ref[name]
+                columns = pl.ds(pl.multiple_of(at * part, part), part)
+                back = b_ref[pl.ds(at * group, group), GRAD, r].reshape(part, d).astype(F32)
+                held[k * part:(k + 1) * part, :] = (back * g_ref[r, columns, :].astype(F32)).astype(BF16)
+            terms = dot(held[...], t_ref[r], NT).astype(BF16)
+            for k, out in enumerate(outs):
+                out[r] = terms[k * part:(k + 1) * part]
+
+    vmem = pl.BlockSpec(memory_space=pltpu.VMEM)
+    return pl.pallas_call(
+        kernel,
+        in_specs=[pl.BlockSpec(memory_space=pltpu.SMEM), vmem, vmem, vmem],
+        out_specs=[vmem] * count,
+        out_shape=[pltpu.VMEM((rows, part, cols), BF16)] * count,
+        scratch_shapes=[pltpu.VMEM((count * part, d), BF16)],
+        compiler_params=params(8),
+        cost_estimate=cost(count * rows * cols * part * d * 2, 2 * count * rows * (cols * part + 2 * part * d)),
     )(place, slabs, tokens, gate_values)
 
 
@@ -184,35 +184,30 @@
     )(slabs, first_blocks, tokens, gate_values)
 
 
-def column_pair(g_ref, k):
-    devices, _, _, both, d = g_ref.shape
-    pair = g_ref[:, 0, k].astype(F32).reshape(devices, 2, both // 2, d)
+def split_pair(pair):
+    devices, both, d = pair.shape
+    pair = pair.astype(F32).reshape(devices, 2, both // 2, d)
     return [pair[:, c].reshape(devices * both // 2, d).astype(BF16) for c in range(2)]
 
 
 def second_terms(place, whose, slabs, cotangent):
     cols, rows, d = cotangent.shape
-    devices, _, pairs, both, _ = slabs.shape
+    _, _, pairs, _, _ = slabs.shape
     step, part = pairs // 4, cols // 4
 
     def kernel(place_ref, g_ref, c_ref, out_ref):
+        at = place_ref[whose]
         for k in range(step):
-            for c, column in enumerate(column_pair(g_ref, k)):
-                out_ref[2 * k + c] = dot(c_ref[2 * k + c], column, NT).astype(BF16)
-
-    return pl.pallas_call(
-        kernel,
-        grid_spec=pltpu.PrefetchScalarGridSpec(
-            num_scalar_prefetch=1,
-            grid=(1,),
-            in_specs=[
-                pl.BlockSpec((devices, 1, step, both, d), lambda i, at: (0, GATED, at[whose], 0, 0)),
-                pl.BlockSpec((part, rows, d), lambda i, at: (at[whose], 0, 0)),
-            ],
-            out_specs=pl.BlockSpec((part, rows, rows), lambda i, at: (0, 0, 0)),
-        ),
-        out_shape=jax.ShapeDtypeStruct((part, rows, rows), BF16),
-        compiler_params=params(24),
+            for c, column in enumerate(split_pair(g_ref[:, GATED, at * step + k])):
+                out_ref[2 * k + c] = dot(c_ref[at * part + 2 * k + c], column, NT).astype(BF16)
+
+    vmem = pl.BlockSpec(memory_space=pltpu.VMEM)
+    return pl.pallas_call(
+        kernel,
+        in_specs=[pl.BlockSpec(memory_space=pltpu.SMEM), vmem, vmem],
+        out_specs=vmem,
+        out_shape=pltpu.VMEM((part, rows, rows), BF16),
+        compiler_params=params(8),
         cost_estimate=cost(2 * part * rows * rows * d, 2 * part * rows * (rows + 2 * d)),
     )(place, slabs, cotangent)
 
@@ -224,7 +219,7 @@
 
     def kernel(g_ref, s_ref, out_ref):
         for k in range(step):
-            for c, column in enumerate(column_pair(g_ref, k)):
+            for c, column in enumerate(split_pair(g_ref[:, 0, k])):
                 out_ref[2 * k + c] = dot(s_ref[2 * k + c], column, NN).astype(BF16)
 
     return pl.pallas_call(
@@ -261,13 +256,12 @@
     slabs, place = after(slabs, place)
     slabs = lax.all_to_all(slabs, "seq", split_axis=0, concat_axis=0, tiled=True)
 
-    def terms(whose):
-        return first_terms(place, whose, slabs, tokens, gate_values), second_terms(place, whose, slabs, cotangent)
-
     def over_cores(whose, whose_beside):
-        first, second = terms(whose_beside)
-        first, second = swap(first, 1), swap(second, 1)
-        near_first, near_second = terms(whose)
+        first, near_first = first_terms(place, (whose_beside, whose), slabs, tokens, gate_values)
+        first, late = after(first, cotangent)
+        first = swap(first, 1)
+        second = swap(second_terms(place, whose_beside, slabs, late), 1)
+        near_second = second_terms(place, whose, slabs, late)
         return add(near_first, first), add(near_second, second)
 
     away = [x.astype(BF16) for x in over_cores(ACROSS, OPPOSITE)]

time: 139 us -> 137 us (0.986)
  Pallas kernels: 29.2 us -> 24.6 us
  waiting for transfers between devices: 14.7 us -> 18.6 us
    pallas_call x8 -> x6, Pallas kernels: 12.3 us -> 7.73 us  [the longest x4 4.03 us: second_terms(): pl.pallas_call(kernel, in_specs=[pl.BlockSpec(memory_space=pltpu.SMEM), v...]
    ppermute x6, waiting for transfers between devices: 14.7 us -> 18.6 us  [swap(): return lax.ppermute(x, 'ch', [(i, i ^ bit) for i in range(4)])]
  transfers between devices with their start and end apart: 6 -> 6, of which waited for: 2 -> 4; matrix products, arithmetic and copies ran while one was open for 1% -> 1% of each run, Pallas kernels for 14% -> 11%
where the time goes in v4:
time: 137 us
  blocking collectives  84.5 us (62%)
  Pallas kernels  24.6 us (18%)
  waiting for transfers between devices  18.6 us (14%)
  starting transfers between devices  5.79 us (4%)
  other arithmetic  2.93 us (2%)
    all_to_all x1, blocking collectives, local(): lax.all_to_all(slabs, 'seq', split_axis=0, concat_axis=0, tiled=True)  84.5 us
    ppermute x6, waiting for transfers between devices, swap(): return lax.ppermute(x, 'ch', [(i, i ^ bit) for i in range(4)])  18.6 us
    pallas_call x1, Pallas kernels, send_slabs(): pl.pallas_call(kernel, in_specs=[hbm] * 5, out_specs=pl.BlockSpec(memory_...  7.5 us
    pallas_call x1, Pallas kernels, row_grads(): pl.pallas_call(kernel, grid=(rows // step,), in_specs=[grad_spec(slabs, s...  6.45 us
    ppermute x6, starting transfers between devices, swap(): return lax.ppermute(x, 'ch', [(i, i ^ bit) for i in range(4)])  5.79 us
    pallas_call x4, Pallas kernels, second_terms(): pl.pallas_call(kernel, in_specs=[pl.BlockSpec(memory_space=pltpu.SMEM), v...  4.03 us
    pallas_call x2, Pallas kernels, first_terms(): pl.pallas_call(kernel, in_specs=[pl.BlockSpec(memory_space=pltpu.SMEM), v...  3.7 us
    pallas_call x1, Pallas kernels, mixed_columns(): pl.pallas_call(kernel, grid=(pairs // step,), in_specs=[pl.BlockSpec((dev...  2.89 us
  transfers between devices with their start and end apart: 6, of which 4 were waited for; matrix products, arithmetic and copies ran while one was open for 1% of the time, Pallas kernels for 11%

profile of v4, /device:TPU:1, one launch (start us, length us, event | category | flops | bytes accessed | tf_op | source)
XLA Modules:
  0.0 137.2 jit_solution(15418935366607315771)
XLA Ops:
  0.7 7.5 %shard_map.92 = bf16[32,2,8,16,384]{4,3,2,1,0:T(8,128)(2,1)S(1)} custom-call(bf16[16,256,256]{2,1,0:T(8,128)(2,1)} %s_ref, bf16[16,256,384]{2,1,0:T(8,128)(2,1)} %c_ref.3, bf16[8,512,512]{2,1,0:T(8,128)(2,1)} %f_ref.1, bf16[8,512,384]{2,1,0:T(8,128)(2,1)} %t_ref.3, bf16[8,512,384]{2,1,0:T(8,128)(2,1)} %g_ref.3), custom_call_target="tpu_custom_call" | custom-call | flops 24159 | bytes 220 | tf_op jit(solution)/shard_map/pallas_call | solution.py:105
  8.2 84.5 %all_to_all.5.b_ref.g_ref = bf16[32,2,8,16,384]{4,3,2,1,0:T(8,128)(2,1)S(1)} all-to-all(bf16[32,2,8,16,384]{4,3,2,1,0:T(8,128)(2,1)S(1)} %shard_map.92), channel_id=1, replica_groups=mesh['seq'=32,'ch'=4] {'seq'}, dimensions={0} | all-to-all | bytes 12582912 | tf_op jit(solution)/shard_map/all_to_all | solution.py:257
  92.8 1.9 %shard_map.93 = (bf16[8,128,512]{2,1,0:T(8,128)(2,1)S(1)}, bf16[8,128,512]{2,1,0:T(8,128)(2,1)S(1)}) custom-call(s32[4]{0:T(128)S(1)} %pad_add_fusion.place_ref, bf16[32,2,8,16,384]{4,3,2,1,0:T(8,128)(2,1)S(1)} %all_to_all.5.b_ref.g_ref, bf16[8,512,384]{2,1,0:T(8,128)(2,1)S(1)} %copy-done.1, bf16[8,512,384]{2,1,0:T(8,128)(2,1)S(1)} %copy-done.2), custom_call_target="tpu_custom_call" | custom-call | flops 8053 | bytes 52 | tf_op jit(solution)/shard_map/pallas_call | solution.py:151
  94.6 1.9 %collective-permute-start = (bf16[8,128,512]{2,1,0:T(8,128)(2,1)S(1)}, bf16[8,128,512]{2,1,0:T(8,128)(2,1)S(1)}, u32[]{:S(2)}, u32[]{:S(2)}) collective-permute-start(bf16[8,128,512]{2,1,0:T(8,128)(2,1)S(1)} %get-tuple-element.31), channel_id=1, source_target_pairs={{0,1},{1,0},{2,3},{3,2},{4,5},{5,4},{6,7},{7,6},{8,9},{9,8},{10,11... | collective-permute-start | bytes 3145736 | tf_op jit(solution)/shard_map/ppermute | solution.py:240
  96.6 1.0 shard_map.95
  97.6 0.1 collective-permute-start.1
  97.7 1.0 shard_map.94
  98.7 0.9 collective-permute-done.1
  99.6 0.1 add_convert_fusion.3
  99.8 0.3 add_convert_fusion.1
  100.1 0.4 collective-permute-start.2
  100.5 1.1 collective-permute-start.5
  101.6 2.9 %shard_map.96 = bf16[16,256,384]{2,1,0:T(8,128)(2,1)} custom-call(bf16[32,2,8,16,384]{4,3,2,1,0:T(8,128)(2,1)S(1)} %all_to_all.5.b_ref.g_ref, bf16[16,256,256]{2,1,0:T(8,128)(2,1)S(1)} %copy-done.4), custom_call_target="tpu_custom_call" | custom-call | flops 8053 | bytes 83 | tf_op jit(solution)/shard_map/pallas_call | solution.py:225
  104.5 8.8 %collective-permute-done.2 = bf16[4,256,256]{2,1,0:T(8,128)(2,1)S(1)} collective-permute-done((bf16[4,256,256]{2,1,0:T(8,128)(2,1)S(1)}, bf16[4,256,256]{2,1,0:T(8,128)(2,1)S(1)}, u32[]{:S(2)}, u32[]{:S(2)}) %collective-permute-start.2) | collective-permute-done | bytes 524320 | tf_op jit(solution)/shard_map/ppermute | solution.py:240
  113.3 1.9 %shard_map.97 = (bf16[8,128,512]{2,1,0:T(8,128)(2,1)S(1)}, bf16[8,128,512]{2,1,0:T(8,128)(2,1)S(1)}) custom-call(s32[4]{0:T(128)S(1)} %pad_add_fusion.place_ref, bf16[32,2,8,16,384]{4,3,2,1,0:T(8,128)(2,1)S(1)} %all_to_all.5.b_ref.g_ref, bf16[8,512,384]{2,1,0:T(8,128)(2,1)S(1)} %copy-done.1, bf16[8,512,384]{2,1,0:T(8,128)(2,1)S(1)} %copy-done.2), custom_call_target="tpu_custom_call" | custom-call | flops 8053 | bytes 52 | tf_op jit(solution)/shard_map/pallas_call | solution.py:151
  115.2 2.1 %collective-permute-start.4 = (bf16[8,128,512]{2,1,0:T(8,128)(2,1)S(1)}, bf16[8,128,512]{2,1,0:T(8,128)(2,1)S(1)}, u32[]{:S(2)}, u32[]{:S(2)}) collective-permute-start(bf16[8,128,512]{2,1,0:T(8,128)(2,1)S(1)} %get-tuple-element.46), channel_id=1, source_target_pairs={{0,1},{1,0},{2,3},{3,2},{4,5},{5,4},{6,7},{7,6},{8,9},{9,8},{10,11... | collective-permute-start | bytes 3145736 | tf_op jit(solution)/shard_map/ppermute | solution.py:240
  117.3 1.0 shard_map.99
  118.3 0.1 collective-permute-start.3
  118.4 1.0 shard_map.98
  119.4 0.9 collective-permute-done.3
  120.3 1.0 add_convert_fusion.2
  121.3 6.5 %shard_map.100 = (bf16[8,512,384]{2,1,0:T(8,128)(2,1)}, bf16[8,512,384]{2,1,0:T(8,128)(2,1)}) custom-call(bf16[32,2,8,16,384]{4,3,2,1,0:T(8,128)(2,1)S(1)} %all_to_all.5.b_ref.g_ref, bf16[8,512,512]{2,1,0:T(8,128)(2,1)S(1)} %copy-done.3, bf16[8,512,384]{2,1,0:T(8,128)(2,1)S(1)} %copy-done.1, bf16[8,512,384]{2,1,0:T(8,128)(2,1)S(1)} %copy-done.2), custom_call_target="tpu_custom_call" | custom-call | flops 32212 | bytes 199 | tf_op jit(solution)/shard_map/pallas_call | solution.py:176
  127.7 8.0 %collective-permute-done.5 = bf16[8,128,512]{2,1,0:T(8,128)(2,1)S(1)} collective-permute-done((bf16[8,128,512]{2,1,0:T(8,128)(2,1)S(1)}, bf16[8,128,512]{2,1,0:T(8,128)(2,1)S(1)}, u32[]{:S(2)}, u32[]{:S(2)}) %collective-permute-start.5) | collective-permute-done | bytes 1048608 | tf_op jit(solution)/shard_map/ppermute | solution.py:240
  135.8 1.4 %add_convert_fusion = bf16[8,128,512]{2,1,0:T(8,128)(2,1)} fusion(bf16[8,128,512]{2,1,0:T(8,128)(2,1)S(1)} %collective-permute-done.5, bf16[8,128,512]{2,1,0:T(8,128)(2,1)S(1)} %collective-permute-done.4, bf16[8,128,512]{2,1,0:T(8,128)(2,1)S(1)} %get-tuple-element.45), kind=kLoop, calls=%fused_computation | loop fusion | flops 3145728 | bytes 4194304 | tf_op jit(solution)/shard_map/convert_element_type | solution.py:277
  (13 shorter events, 0.1 us)
Async XLA Ops:
  8.2 84.5 %copy-start.1 = (bf16[8,512,384]{2,1,0:T(8,128)(2,1)S(1)}, bf16[8,512,384]{2,1,0:T(8,128)(2,1)}, u32[]{:S(2)}) copy-start(bf16[8,512,384]{2,1,0:T(8,128)(2,1)} %t_ref.3) | copy-start | bytes 9437188
  8.2 84.5 %copy-start.2 = (bf16[8,512,384]{2,1,0:T(8,128)(2,1)S(1)}, bf16[8,512,384]{2,1,0:T(8,128)(2,1)}, u32[]{:S(2)}) copy-start(bf16[8,512,384]{2,1,0:T(8,128)(2,1)} %g_ref.3) | copy-start | bytes 9437188
  92.8 3.8 %copy-start = (bf16[16,256,384]{2,1,0:T(8,128)(2,1)S(1)}, bf16[16,256,384]{2,1,0:T(8,128)(2,1)}, u32[]{:S(2)}) copy-start(bf16[16,256,384]{2,1,0:T(8,128)(2,1)} %c_ref.3) | copy-start | bytes 9437188
  94.6 5.1 %collective-permute-start = (bf16[8,128,512]{2,1,0:T(8,128)(2,1)S(1)}, bf16[8,128,512]{2,1,0:T(8,128)(2,1)S(1)}, u32[]{:S(2)}, u32[]{:S(2)}) collective-permute-start(bf16[8,128,512]{2,1,0:T(8,128)(2,1)S(1)} %get-tuple-element.31), channel_id=1, source_target_pairs={{0,1},{1,0},{2,3},{3,2},{4,5},{5,4},{6,7},{7,6},{8,9},{9,8},{10,11... | collective-permute-start | bytes 3145736 | tf_op jit(solution)/shard_map/ppermute | solution.py:240
  97.6 2.0 %collective-permute-start.1 = (bf16[4,256,256]{2,1,0:T(8,128)(2,1)S(1)}, bf16[4,256,256]{2,1,0:T(8,128)(2,1)S(1)}, u32[]{:S(2)}, u32[]{:S(2)}) collective-permute-start(bf16[4,256,256]{2,1,0:T(8,128)(2,1)S(1)} %shard_map.95), channel_id=1, source_target_pairs={{0,1},{1,0},{2,3},{3,2},{4,5},{5,4},{6,7},{7,6},{8,9},{9,8},{10,11... | collective-permute-start | bytes 1572872 | tf_op jit(solution)/shard_map/ppermute | solution.py:240
  98.7 2.9 %copy-start.4 = (bf16[16,256,256]{2,1,0:T(8,128)(2,1)S(1)}, bf16[16,256,256]{2,1,0:T(8,128)(2,1)}, u32[]{:S(2)}) copy-start(bf16[16,256,256]{2,1,0:T(8,128)(2,1)} %s_ref) | copy-start | bytes 6291460
  100.1 13.2 %collective-permute-start.2 = (bf16[4,256,256]{2,1,0:T(8,128)(2,1)S(1)}, bf16[4,256,256]{2,1,0:T(8,128)(2,1)S(1)}, u32[]{:S(2)}, u32[]{:S(2)}) collective-permute-start(bf16[4,256,256]{2,1,0:T(8,128)(2,1)S(1)} %add_convert_fusion.3), channel_id=1, source_target_pairs={{0,2},{1,3},{2,0},{3,1},{4,6},{5,7},{6,4},{7,5},{8,10},{9,11},{10,... | collective-permute-start | bytes 1572872 | tf_op jit(solution)/shard_map/ppermute | solution.py:240
  100.5 35.2 %collective-permute-start.5 = (bf16[8,128,512]{2,1,0:T(8,128)(2,1)S(1)}, bf16[8,128,512]{2,1,0:T(8,128)(2,1)S(1)}, u32[]{:S(2)}, u32[]{:S(2)}) collective-permute-start(bf16[8,128,512]{2,1,0:T(8,128)(2,1)S(1)} %add_convert_fusion.1), channel_id=1, source_target_pairs={{0,2},{1,3},{2,0},{3,1},{4,6},{5,7},{6,4},{7,5},{8,10},{9,11},{10,... | collective-permute-start | bytes 3145736 | tf_op jit(solution)/shard_map/ppermute | solution.py:240
  115.2 20.6 %collective-permute-start.4 = (bf16[8,128,512]{2,1,0:T(8,128)(2,1)S(1)}, bf16[8,128,512]{2,1,0:T(8,128)(2,1)S(1)}, u32[]{:S(2)}, u32[]{:S(2)}) collective-permute-start(bf16[8,128,512]{2,1,0:T(8,128)(2,1)S(1)} %get-tuple-element.46), channel_id=1, source_target_pairs={{0,1},{1,0},{2,3},{3,2},{4,5},{5,4},{6,7},{7,6},{8,9},{9,8},{10,11... | collective-permute-start | bytes 3145736 | tf_op jit(solution)/shard_map/ppermute | solution.py:240
  118.3 2.0 %collective-permute-start.3 = (bf16[4,256,256]{2,1,0:T(8,128)(2,1)S(1)}, bf16[4,256,256]{2,1,0:T(8,128)(2,1)S(1)}, u32[]{:S(2)}, u32[]{:S(2)}) collective-permute-start(bf16[4,256,256]{2,1,0:T(8,128)(2,1)S(1)} %shard_map.99), channel_id=1, source_target_pairs={{0,1},{1,0},{2,3},{3,2},{4,5},{5,4},{6,7},{7,6},{8,9},{9,8},{10,11... | collective-permute-start | bytes 1572872 | tf_op jit(solution)/shard_map/ppermute | solution.py:240
  118.4 2.9 %copy-start.3 = (bf16[8,512,512]{2,1,0:T(8,128)(2,1)S(1)}, bf16[8,512,512]{2,1,0:T(8,128)(2,1)}, u32[]{:S(2)}) copy-start(bf16[8,512,512]{2,1,0:T(8,128)(2,1)} %f_ref.1) | copy-start | bytes 12582916

commit v5 on v4

--- a/solution.py
+++ b/solution.py
@@ -240,6 +240,23 @@
     return lax.ppermute(x, "ch", [(i, i ^ bit) for i in range(4)])
 
 
+def near_sum(near, beside):
+    vmem = pl.BlockSpec(memory_space=pltpu.VMEM)
+
+    def kernel(a_ref, b_ref, out_ref):
+        for r in range(near.shape[0]):
+            out_ref[r] = add(a_ref[r], b_ref[r])
+
+    return pl.pallas_call(
+        kernel,
+        in_specs=[vmem] * 2,
+        out_specs=vmem,
+        out_shape=pltpu.VMEM(near.shape, F32),
+        compiler_params=params(8),
+        cost_estimate=cost(near.size, 8 * near.size),
+    )(near, beside)
+
+
 def add(a, b):
     return a.astype(F32) + b.astype(F32)
 
@@ -262,9 +279,10 @@
         first = swap(first, 1)
         second = swap(second_terms(place, whose_beside, slabs, late), 1)
         near_second = second_terms(place, whose, slabs, late)
-        return add(near_first, first), add(near_second, second)
-
-    away = [x.astype(BF16) for x in over_cores(ACROSS, OPPOSITE)]
+        return (near_first, first), add(near_second, second)
+
+    first, second = over_cores(ACROSS, OPPOSITE)
+    away = [add(*first).astype(BF16), second.astype(BF16)]
     *away, second_blocks = after(*away, second_blocks)
     across_c, across_b = swap(away[1], 2), swap(away[0], 2)
     mixed_output = mixed_columns(slabs, second_blocks)
@@ -272,7 +290,8 @@
         across_c, mixed_output, tokens, gate_values, cotangent
     )
     here_b, here_c = over_cores(HERE, BESIDE)
-    second_grad, gate_values = after((here_c + across_c.astype(F32)).astype(BF16), gate_values)
+    here_b = near_sum(*here_b)
+    second_grad, here_b, gate_values = after((here_c + across_c.astype(F32)).astype(BF16), here_b, gate_values)
     token_grad, gate_grad = row_grads(slabs, first_blocks, tokens, gate_values)
     first_grad = (here_b + across_b.astype(F32)).astype(BF16)
     return (mixed_output, token_grad, gate_grad, first_grad, second_grad)

time: 137 us -> 143 us (1.044)
  waiting for transfers between devices: 18.6 us -> 24.3 us
    ppermute x6, waiting for transfers between devices: 18.6 us -> 24.3 us  [swap(): return lax.ppermute(x, 'ch', [(i, i ^ bit) for i in range(4)])]
  transfers between devices with their start and end apart: 6 -> 6, of which waited for: 4 -> 4; matrix products, arithmetic and copies ran while one was open for 1% -> 1% of each run, Pallas kernels for 11% -> 10%
where the time goes in v5:
time: 143 us; the launch traced here: 142 us
  blocking collectives  84.5 us (59%)
  Pallas kernels  24.8 us (17%)
  waiting for transfers between devices  24.3 us (17%)
  starting transfers between devices  4.58 us (3%)
  other arithmetic  2.83 us (2%)
    all_to_all x1, blocking collectives, local(): lax.all_to_all(slabs, 'seq', split_axis=0, concat_axis=0, tiled=True)  84.5 us
    ppermute x6, waiting for transfers between devices, swap(): return lax.ppermute(x, 'ch', [(i, i ^ bit) for i in range(4)])  24.3 us
    pallas_call x1, Pallas kernels, send_slabs(): pl.pallas_call(kernel, in_specs=[hbm] * 5, out_specs=pl.BlockSpec(memory_...  7.5 us
    pallas_call x1, Pallas kernels, row_grads(): pl.pallas_call(kernel, grid=(rows // step,), in_specs=[grad_spec(slabs, s...  6.45 us
    ppermute x6, starting transfers between devices, swap(): return lax.ppermute(x, 'ch', [(i, i ^ bit) for i in range(4)])  4.58 us
    pallas_call x4, Pallas kernels, second_terms(): pl.pallas_call(kernel, in_specs=[pl.BlockSpec(memory_space=pltpu.SMEM), v...  4.02 us
    pallas_call x2, Pallas kernels, first_terms(): pl.pallas_call(kernel, in_specs=[pl.BlockSpec(memory_space=pltpu.SMEM), v...  3.7 us
    pallas_call x1, Pallas kernels, mixed_columns(): pl.pallas_call(kernel, grid=(pairs // step,), in_specs=[pl.BlockSpec((dev...  2.9 us
  transfers between devices with their start and end apart: 6, of which 4 were waited for; matrix products, arithmetic and copies ran while one was open for 1% of the time, Pallas kernels for 10%

profile of v5, /device:TPU:1, one launch (start us, length us, event | category | flops | bytes accessed | tf_op | source)
XLA Modules:
  0.0 142.5 jit_solution(2301817287801989135)
XLA Ops:
  0.7 7.5 %shard_map.92 = bf16[32,2,8,16,384]{4,3,2,1,0:T(8,128)(2,1)S(1)} custom-call(bf16[16,256,256]{2,1,0:T(8,128)(2,1)} %s_ref, bf16[16,256,384]{2,1,0:T(8,128)(2,1)} %c_ref.3, bf16[8,512,512]{2,1,0:T(8,128)(2,1)} %f_ref.1, bf16[8,512,384]{2,1,0:T(8,128)(2,1)} %t_ref.3, bf16[8,512,384]{2,1,0:T(8,128)(2,1)} %g_ref.3), custom_call_target="tpu_custom_call" | custom-call | flops 24159 | bytes 220 | tf_op jit(solution)/shard_map/pallas_call | solution.py:105
  8.2 84.5 %all_to_all.5.b_ref.g_ref = bf16[32,2,8,16,384]{4,3,2,1,0:T(8,128)(2,1)S(1)} all-to-all(bf16[32,2,8,16,384]{4,3,2,1,0:T(8,128)(2,1)S(1)} %shard_map.92), channel_id=1, replica_groups=mesh['seq'=32,'ch'=4] {'seq'}, dimensions={0} | all-to-all | bytes 12582912 | tf_op jit(solution)/shard_map/all_to_all | solution.py:274
  92.8 1.9 %shard_map.93 = (bf16[8,128,512]{2,1,0:T(8,128)(2,1)S(1)}, bf16[8,128,512]{2,1,0:T(8,128)(2,1)S(1)}) custom-call(s32[4]{0:T(128)S(1)} %pad_add_fusion.place_ref, bf16[32,2,8,16,384]{4,3,2,1,0:T(8,128)(2,1)S(1)} %all_to_all.5.b_ref.g_ref, bf16[8,512,384]{2,1,0:T(8,128)(2,1)S(1)} %copy-done.1, bf16[8,512,384]{2,1,0:T(8,128)(2,1)S(1)} %copy-done.2), custom_call_target="tpu_custom_call" | custom-call | flops 8053 | bytes 52 | tf_op jit(solution)/shard_map/pallas_call | solution.py:151
  94.6 1.9 %collective-permute-start = (bf16[8,128,512]{2,1,0:T(8,128)(2,1)S(1)}, bf16[8,128,512]{2,1,0:T(8,128)(2,1)S(1)}, u32[]{:S(2)}, u32[]{:S(2)}) collective-permute-start(bf16[8,128,512]{2,1,0:T(8,128)(2,1)S(1)} %get-tuple-element.32), channel_id=1, source_target_pairs={{0,1},{1,0},{2,3},{3,2},{4,5},{5,4},{6,7},{7,6},{8,9},{9,8},{10,11... | collective-permute-start | bytes 3145736 | tf_op jit(solution)/shard_map/ppermute | solution.py:240
  96.6 1.0 shard_map.95
  97.7 1.0 shard_map.94
  98.7 0.9 collective-permute-done.1
  99.8 0.3 add_convert_fusion.1
  100.1 0.4 collective-permute-start.2
  100.5 2.9 %shard_map.96 = bf16[16,256,384]{2,1,0:T(8,128)(2,1)} custom-call(bf16[32,2,8,16,384]{4,3,2,1,0:T(8,128)(2,1)S(1)} %all_to_all.5.b_ref.g_ref, bf16[16,256,256]{2,1,0:T(8,128)(2,1)S(1)} %copy-done.4), custom_call_target="tpu_custom_call" | custom-call | flops 8053 | bytes 83 | tf_op jit(solution)/shard_map/pallas_call | solution.py:225
  103.4 9.9 %collective-permute-done.2 = bf16[4,256,256]{2,1,0:T(8,128)(2,1)S(1)} collective-permute-done((bf16[4,256,256]{2,1,0:T(8,128)(2,1)S(1)}, bf16[4,256,256]{2,1,0:T(8,128)(2,1)S(1)}, u32[]{:S(2)}, u32[]{:S(2)}) %collective-permute-start.2) | collective-permute-done | bytes 524320 | tf_op jit(solution)/shard_map/ppermute | solution.py:240
  113.3 1.9 %shard_map.97 = (bf16[8,128,512]{2,1,0:T(8,128)(2,1)S(1)}, bf16[8,128,512]{2,1,0:T(8,128)(2,1)S(1)}) custom-call(s32[4]{0:T(128)S(1)} %pad_add_fusion.place_ref, bf16[32,2,8,16,384]{4,3,2,1,0:T(8,128)(2,1)S(1)} %all_to_all.5.b_ref.g_ref, bf16[8,512,384]{2,1,0:T(8,128)(2,1)S(1)} %copy-done.1, bf16[8,512,384]{2,1,0:T(8,128)(2,1)S(1)} %copy-done.2), custom_call_target="tpu_custom_call" | custom-call | flops 8053 | bytes 52 | tf_op jit(solution)/shard_map/pallas_call | solution.py:151
  115.1 1.3 collective-permute-start.4
  116.4 0.4 collective-permute-start.5
  116.8 1.0 shard_map.99
  117.8 0.4 collective-permute-start.3
  118.3 1.0 shard_map.98
  119.3 0.5 collective-permute-done.3
  119.8 1.0 add_convert_fusion.2
  120.8 0.2 shard_map.100
  121.0 0.6 copy-done.3
  121.6 6.4 %shard_map.101 = (bf16[8,512,384]{2,1,0:T(8,128)(2,1)}, bf16[8,512,384]{2,1,0:T(8,128)(2,1)}) custom-call(bf16[32,2,8,16,384]{4,3,2,1,0:T(8,128)(2,1)S(1)} %all_to_all.5.b_ref.g_ref, bf16[8,512,512]{2,1,0:T(8,128)(2,1)S(1)} %copy-done.3, bf16[8,512,384]{2,1,0:T(8,128)(2,1)S(1)} %copy-done.1, bf16[8,512,384]{2,1,0:T(8,128)(2,1)S(1)} %copy-done.2), custom_call_target="tpu_custom_call" | custom-call | flops 32212 | bytes 199 | tf_op jit(solution)/shard_map/pallas_call | solution.py:176
  128.1 13.0 %collective-permute-done.5 = bf16[8,128,512]{2,1,0:T(8,128)(2,1)S(1)} collective-permute-done((bf16[8,128,512]{2,1,0:T(8,128)(2,1)S(1)}, bf16[8,128,512]{2,1,0:T(8,128)(2,1)S(1)}, u32[]{:S(2)}, u32[]{:S(2)}) %collective-permute-start.5) | collective-permute-done | bytes 1048608 | tf_op jit(solution)/shard_map/ppermute | solution.py:240
  141.1 1.3 add_convert_fusion
  (14 shorter events, 0.3 us)
Async XLA Ops:
  8.2 84.5 %copy-start.1 = (bf16[8,512,384]{2,1,0:T(8,128)(2,1)S(1)}, bf16[8,512,384]{2,1,0:T(8,128)(2,1)}, u32[]{:S(2)}) copy-start(bf16[8,512,384]{2,1,0:T(8,128)(2,1)} %t_ref.3) | copy-start | bytes 9437188
  8.2 84.5 %copy-start.2 = (bf16[8,512,384]{2,1,0:T(8,128)(2,1)S(1)}, bf16[8,512,384]{2,1,0:T(8,128)(2,1)}, u32[]{:S(2)}) copy-start(bf16[8,512,384]{2,1,0:T(8,128)(2,1)} %g_ref.3) | copy-start | bytes 9437188
  92.8 3.8 %copy-start = (bf16[16,256,384]{2,1,0:T(8,128)(2,1)S(1)}, bf16[16,256,384]{2,1,0:T(8,128)(2,1)}, u32[]{:S(2)}) copy-start(bf16[16,256,384]{2,1,0:T(8,128)(2,1)} %c_ref.3) | copy-start | bytes 9437188
  94.6 5.1 %collective-permute-start = (bf16[8,128,512]{2,1,0:T(8,128)(2,1)S(1)}, bf16[8,128,512]{2,1,0:T(8,128)(2,1)S(1)}, u32[]{:S(2)}, u32[]{:S(2)}) collective-permute-start(bf16[8,128,512]{2,1,0:T(8,128)(2,1)S(1)} %get-tuple-element.32), channel_id=1, source_target_pairs={{0,1},{1,0},{2,3},{3,2},{4,5},{5,4},{6,7},{7,6},{8,9},{9,8},{10,11... | collective-permute-start | bytes 3145736 | tf_op jit(solution)/shard_map/ppermute | solution.py:240
  97.6 2.0 %collective-permute-start.1 = (bf16[4,256,256]{2,1,0:T(8,128)(2,1)S(1)}, bf16[4,256,256]{2,1,0:T(8,128)(2,1)S(1)}, u32[]{:S(2)}, u32[]{:S(2)}) collective-permute-start(bf16[4,256,256]{2,1,0:T(8,128)(2,1)S(1)} %shard_map.95), channel_id=1, source_target_pairs={{0,1},{1,0},{2,3},{3,2},{4,5},{5,4},{6,7},{7,6},{8,9},{9,8},{10,11... | collective-permute-start | bytes 1572872 | tf_op jit(solution)/shard_map/ppermute | solution.py:240
  98.7 1.8 %copy-start.4 = (bf16[16,256,256]{2,1,0:T(8,128)(2,1)S(1)}, bf16[16,256,256]{2,1,0:T(8,128)(2,1)}, u32[]{:S(2)}) copy-start(bf16[16,256,256]{2,1,0:T(8,128)(2,1)} %s_ref) | copy-start | bytes 6291460
  100.1 13.2 %collective-permute-start.2 = (bf16[4,256,256]{2,1,0:T(8,128)(2,1)S(1)}, bf16[4,256,256]{2,1,0:T(8,128)(2,1)S(1)}, u32[]{:S(2)}, u32[]{:S(2)}) collective-permute-start(bf16[4,256,256]{2,1,0:T(8,128)(2,1)S(1)} %add_convert_fusion.3), channel_id=1, source_target_pairs={{0,2},{1,3},{2,0},{3,1},{4,6},{5,7},{6,4},{7,5},{8,10},{9,11},{10,... | collective-permute-start | bytes 1572872 | tf_op jit(solution)/shard_map/ppermute | solution.py:240
  115.1 5.6 %collective-permute-start.4 = (bf16[8,128,512]{2,1,0:T(8,128)(2,1)S(1)}, bf16[8,128,512]{2,1,0:T(8,128)(2,1)S(1)}, u32[]{:S(2)}, u32[]{:S(2)}) collective-permute-start(bf16[8,128,512]{2,1,0:T(8,128)(2,1)S(1)} %get-tuple-element.44), channel_id=1, source_target_pairs={{0,1},{1,0},{2,3},{3,2},{4,5},{5,4},{6,7},{7,6},{8,9},{9,8},{10,11... | collective-permute-start | bytes 3145736 | tf_op jit(solution)/shard_map/ppermute | solution.py:240
  116.4 24.7 %collective-permute-start.5 = (bf16[8,128,512]{2,1,0:T(8,128)(2,1)S(1)}, bf16[8,128,512]{2,1,0:T(8,128)(2,1)S(1)}, u32[]{:S(2)}, u32[]{:S(2)}) collective-permute-start(bf16[8,128,512]{2,1,0:T(8,128)(2,1)S(1)} %add_convert_fusion.1), channel_id=1, source_target_pairs={{0,2},{1,3},{2,0},{3,1},{4,6},{5,7},{6,4},{7,5},{8,10},{9,11},{10,... | collective-permute-start | bytes 3145736 | tf_op jit(solution)/shard_map/ppermute | solution.py:240
  117.8 2.0 %collective-permute-start.3 = (bf16[4,256,256]{2,1,0:T(8,128)(2,1)S(1)}, bf16[4,256,256]{2,1,0:T(8,128)(2,1)S(1)}, u32[]{:S(2)}, u32[]{:S(2)}) collective-permute-start(bf16[4,256,256]{2,1,0:T(8,128)(2,1)S(1)} %shard_map.99), channel_id=1, source_target_pairs={{0,1},{1,0},{2,3},{3,2},{4,5},{5,4},{6,7},{7,6},{8,9},{9,8},{10,11... | collective-permute-start | bytes 1572872 | tf_op jit(solution)/shard_map/ppermute | solution.py:240
  119.3 2.4 %copy-start.3 = (bf16[8,512,512]{2,1,0:T(8,128)(2,1)S(1)}, bf16[8,512,512]{2,1,0:T(8,128)(2,1)}, u32[]{:S(2)}) copy-start(bf16[8,512,512]{2,1,0:T(8,128)(2,1)} %f_ref.1) | copy-start | bytes 12582916
